TPU v7x, 32 devices: a whole 2x2x4 slice. The times are simulated.
32 devices in a mesh: group: 2 (over y), ctx: 4 (over z), tp: 2 (over x), rep: 2 (over core).
Axes of the slice: x: 2, y: 2, z: 4, core: 2. Of those that a mesh axis runs over, the one named last changes fastest.
Arguments:
- tokens: bfloat16 [1024, 8192], P(('group', 'ctx')), parts along dimension 0, may hold values from -6 to 6
- adapter_down: bfloat16 [32, 8192, 48], P(('group', 'ctx', 'rep')), parts along dimension 0, may hold values from -0.0625 to 0.0625
- adapter_query: bfloat16 [32, 16, 8, 8, 128], P(('group', 'ctx'), None, ('tp', 'rep')), parts along dimension 0, may hold values from -1.5 to 1.5
- adapter_keyvalue: bfloat16 [32, 16, 2, 8, 128], P(('group', 'ctx'), None, None, ('tp', 'rep')), parts along dimension 0, may hold values from -1.5 to 1.5
- query_base: bfloat16 [1024, 8, 8, 128], P(('group', 'ctx'), ('tp', 'rep')), parts along dimension 0, may hold values from -8 to 8
- keyvalue_base: bfloat16 [1024, 2, 8, 128], P(('group', 'ctx'), None, ('tp', 'rep')), parts along dimension 0, may hold values from -6 to 6
- cached_keys: bfloat16 [4096, 8, 128], P(('group', 'ctx'), ('tp', 'rep')), parts along dimension 0, may hold values from -8 to 8
- cached_values: bfloat16 [4096, 8, 128], P(('group', 'ctx'), ('tp', 'rep')), parts along dimension 0, may hold values from -6 to 6
- adapter_slot: int32 [8, 128], P(('group', 'ctx')), parts along dimension 0, may hold values from 0 to 3, never falling along the last dimension, each value on 1 to 64 neighbouring positions
- cached_length: int32 [8], P('group'), parts along dimension 0, may hold values from 1 to 512, 1280 in all
Outputs:
- attended: bfloat16 [1024, 8, 8, 128], P(('group', 'ctx'), ('tp', 'rep')), parts along dimension 0
There are 2 independent parts, one for each index of `group`. A program takes and returns all parts, laid end to end along the dimension named above; each array names one. Nothing has to cross between parts.
Inputs may be any that keep to these rules, and one draw needn't show every extreme that they name: `adapter_slot`: non-decreasing along each row; every row uses each of its 4 adapters. `cached_length`: some shard is full.
All inputs are finite; a program needn't handle non-finite values.
Results may differ from a plain program's by a relative error of at most 0.012.
Values may be sent and summed in bfloat16 or wider, within the bound.
A program may use at most 64 MiB of HBM per device.

v0:
```python
import jax
import jax.numpy as jnp
from jax import lax
from jax.sharding import PartitionSpec as P

NEGATIVE_FILL = -1e30


def from_partner(value, axis, bit):
    return lax.ppermute(value, axis, [(i, i ^ 1 << bit) for i in range(lax.axis_size(axis))])


def from_behind(value, axis, by):
    devices = lax.axis_size(axis)
    return lax.ppermute(value, axis, [(i, (i + by) % devices) for i in range(devices)])


def order_pair(lower_side, own_part, other_part):
    first_half = jnp.where(lower_side, own_part, other_part)
    second_half = jnp.where(lower_side, other_part, own_part)
    return jnp.concatenate([first_half, second_half], axis=0)


def per_device(
    tokens,
    adapter_down,
    adapter_query,
    adapter_keyvalue,
    query_base,
    keyvalue_base,
    cached_keys,
    cached_values,
    adapter_slot,
    cached_length,
):
    tok_rows = tokens.shape[0]
    slot_count = adapter_query.shape[0]
    rank_cols = adapter_query.shape[1]
    cache_rows = cached_keys.shape[0]
    head_dim = query_base.shape[3]
    lower_side = lax.axis_index("rep") == 0
    partner_stack = from_partner(adapter_down, "rep", 0)
    own_part = jnp.einsum(
        "td,sdk->stk", tokens, adapter_down, preferred_element_type=jnp.float32
    ).astype(jnp.bfloat16)
    other_part = jnp.einsum(
        "td,sdk->stk", tokens, partner_stack, preferred_element_type=jnp.float32
    ).astype(jnp.bfloat16)
    shrunk = order_pair(lower_side, own_part, other_part)
    selector = adapter_slot[0][None, :] == jnp.arange(slot_count, dtype=jnp.int32)[:, None]
    masked = jnp.where(selector[:, :, None], shrunk, jnp.zeros_like(shrunk))
    delta_query = jnp.einsum(
        "str,srhgd->thgd",
        masked[:, :, :rank_cols],
        adapter_query,
        preferred_element_type=jnp.float32,
    )
    query_rows = (query_base.astype(jnp.float32) + delta_query).astype(jnp.bfloat16)
    keyvalue_part = masked[:, :, rank_cols:].reshape(slot_count, tok_rows, 2, rank_cols)
    delta_keyvalue = jnp.einsum(
        "stcr,srchd->tchd", keyvalue_part, adapter_keyvalue, preferred_element_type=jnp.float32
    )
    fresh_rows = (keyvalue_base.astype(jnp.float32) + delta_keyvalue).astype(jnp.bfloat16)
    own_keys = jnp.concatenate([cached_keys, fresh_rows[:, 0]], axis=0)
    own_values = jnp.concatenate([cached_values, fresh_rows[:, 1]], axis=0)
    context_index = lax.axis_index("ctx")
    cycle_size = lax.axis_size("ctx")
    score_scale = head_dim ** (-0.5)
    block_rows = cache_rows + tok_rows
    shard_ids = jnp.arange(cycle_size, dtype=jnp.int32)
    query_position = context_index * tok_rows + jnp.arange(tok_rows, dtype=jnp.int32)

    def attend(carry_state, key_block, value_block, row_start):
        running_max, running_sum, weighted_sum = carry_state
        global_rows = row_start + jnp.arange(key_block.shape[0], dtype=jnp.int32)
        source_shard = global_rows // block_rows
        local_rows = global_rows % block_rows
        length_limit = jnp.sum(
            jnp.where(source_shard[:, None] == shard_ids[None, :], cached_length[None, :], 0),
            axis=1,
        )
        span_position = source_shard * tok_rows + local_rows - cache_rows
        visible = jnp.where(
            (local_rows < cache_rows)[None, :],
            (local_rows < length_limit)[None, :],
            span_position[None, :] <= query_position[:, None],
        )
        scores = (
            jnp.einsum("thgd,lhd->hgtl", query_rows, key_block, preferred_element_type=jnp.float32)
            * score_scale
        )
        scores = jnp.where(visible, scores, NEGATIVE_FILL)
        new_max = jnp.maximum(running_max, jnp.max(scores, axis=-1))
        weights = jnp.where(visible, jnp.exp(scores - new_max[..., None]), 0.0)
        factor = jnp.exp(running_max - new_max)
        running_sum = running_sum * factor + jnp.sum(weights, axis=-1)
        weighted_sum = weighted_sum * factor[..., None] + jnp.einsum(
            "hgtl,lhd->hgtd",
            weights.astype(jnp.bfloat16),
            value_block,
            preferred_element_type=jnp.float32,
        )
        return (new_max, running_sum, weighted_sum)

    head_count = query_rows.shape[1]
    group_count = query_rows.shape[2]
    start_state = (
        jnp.full((head_count, group_count, tok_rows), NEGATIVE_FILL, jnp.float32),
        jnp.zeros((head_count, group_count, tok_rows), jnp.float32),
        jnp.zeros((head_count, group_count, tok_rows, head_dim), jnp.float32),
    )
    carry_state = attend(start_state, own_keys, own_values, context_index * block_rows)

    def cycle_step(step_index, carry):
        state_now, key_block, value_block = carry
        key_block, value_block = from_behind((key_block, value_block), "ctx", 1)
        state_now = attend(
            state_now,
            key_block,
            value_block,
            (context_index - step_index) % cycle_size * block_rows,
        )
        return (state_now, key_block, value_block)

    carry_state, _, _ = lax.fori_loop(
        1, cycle_size, cycle_step, (carry_state, own_keys, own_values)
    )
    running_max, running_sum, weighted_sum = carry_state
    output = weighted_sum / running_sum[..., None]
    return jnp.transpose(output, (2, 0, 1, 3)).astype(jnp.bfloat16)


def solution(mesh):
    in_specs = (
        P(("group", "ctx"), None),
        P(("group", "ctx", "rep"), None, None),
        P(("group", "ctx"), None, ("tp", "rep"), None, None),
        P(("group", "ctx"), None, None, ("tp", "rep"), None),
        P(("group", "ctx"), ("tp", "rep"), None, None),
        P(("group", "ctx"), None, ("tp", "rep"), None),
        P(("group", "ctx"), ("tp", "rep"), None),
        P(("group", "ctx"), ("tp", "rep"), None),
        P(("group", "ctx"), None),
        P("group"),
    )
    out_specs = P(("group", "ctx"), ("tp", "rep"), None, None)
    return jax.shard_map(
        per_device, mesh=mesh, in_specs=in_specs, out_specs=out_specs, check_vma=False
    )
```

profile of v0, /device:TPU:0, one launch (start us, length us, event | category | flops | bytes accessed | tf_op | source)
XLA Modules:
  0.0 86.1 jit_solution(1256597758610815552)
XLA Ops:
  0.0 0.0 copy-start
  0.0 0.0 copy-start.3
  0.0 0.5 collective-permute-start.2
  0.5 1.2 %copy.26 = bf16[512,2,128]{2,0,1:T(8,128)(2,1)S(1)} copy(bf16[512,2,128]{2,1,0:T(2,128)(2,1)} %param.18) | data formatting | bytes 524288 | tf_op args[6]
  1.8 1.0 %copy.29 = bf16[512,2,128]{2,0,1:T(8,128)(2,1)S(1)} copy(bf16[512,2,128]{2,1,0:T(2,128)(2,1)} %param.19) | data formatting | bytes 524288 | tf_op args[7]
  2.8 0.7 select_reduce_fusion.1
  3.6 0.7 iota_compare_fusion.2
  4.3 0.3 compare_select_fusion.1
  4.6 0.0 copy-done
  4.6 2.2 %fusion.43 = bf16[2,48,128]{2,1,0:T(8,128)(2,1)S(1)} fusion(bf16[2,8192,48]{1,2,0:T(8,128)(2,1)} %param.13, bf16[128,8192]{1,0:T(8,128)(2,1)S(1)} %copy-done), kind=kOutput, calls=%fused_computation.52 | convolution fusion | flops 201338880 | bytes 3694592 | tf_op jit(solution)/shard_map/td,sdk->stk/dot_general | solution.py:43
  6.8 0.0 collective-permute-done.2
  6.8 2.2 %select_bitcast_fusion.1 = (bf16[2,128,48]{1,2,0:T(8,128)(2,1)S(1)}, bf16[2,128,48]{1,2,0:T(8,128)(2,1)S(1)}) fusion(bf16[2,48,128]{2,1,0:T(8,128)(2,1)S(1)} %fusion.43, pred[]{:T(512)S(6)} %eq.107, bf16[2,8192,48]{1,2,0:T(8,128)(2,1)} %collective-permute-done.2, bf16[128,8192]{1,0:T(8,128)(2,1)S(1)} %copy-done), kind=kOutput, calls=%fused_computation.70 | convolution fusion | flops 201363456 | bytes 3743745 | tf_op jit(solution)/shard_map/td,sdk->stk/dot_general | solution.py:46
  9.1 0.0 copy-done.6
  9.1 0.0 copy-done.5
  9.1 0.2 fusion.42
  9.3 0.0 copy-done.4
  9.3 0.0 copy-done.3
  9.4 0.3 fusion.40
  9.7 0.9 %fusion.26 = (f32[2,8,128]{2,1,0:T(8,128)S(1)}, f32[2,640,128,8]{2,1,3,0:T(8,128)S(1)}) fusion(pred[128,640]{0,1:T(8,128)(4,1)S(1)} %compare_select_fusion.1, bf16[128,2,8,128]{3,0,2,1:T(8,128)(2,1)S(1)} %fusion.40, bf16[128,2,128]{2,0,1:T(8,128)(2,1)S(1)} %get-tuple-element.366, bf16[512,2,128]{2,0,1:T(8,128)(2,1)S(1)} %copy.26), kind=kOutput, calls=%fused_computation.36 | convolution fusion | flops 340129792 | bytes 6184960 | tf_op jit(solution)/shard_map/thgd,lhd->hgtl/dot_general | solution.py:89
  10.6 1.3 %fusion.28 = f32[2,8,128]{2,1,0:T(8,128)S(1)} fusion(f32[2,640,128,8]{2,1,3,0:T(8,128)S(1)} %get-tuple-element.372, f32[2,8,128]{2,1,0:T(8,128)S(1)} %broadcast_maximum_fusion, pred[128,640]{0,1:T(8,128)(4,1)S(1)} %compare_select_fusion.1), kind=kLoop, calls=%fused_computation.38 | loop fusion | flops 6551552 | bytes 5341184 | tf_op jit(solution)/shard_map/reduce_sum | solution.py:96
  11.9 0.9 %pad_maximum_fusion = (bf16[640,2,128]{2,0,1:T(8,128)(2,1)}, bf16[640,2,128]{2,0,1:T(8,128)(2,1)}) fusion(bf16[128,2,128]{2,0,1:T(8,128)(2,1)S(1)} %get-tuple-element.366, bf16[512,2,128]{2,0,1:T(8,128)(2,1)S(1)} %copy.26, bf16[128,2,128]{2,0,1:T(8,128)(2,1)S(1)} %get-tuple-element.365, bf16[512,2,128]{2,0,1:T(8,128)(2,1)S(1)} %copy.29), kind=kLoop, calls=%fused_computation.57 | loop fusion | flops 1310720 | bytes 1310720 | tf_op jit(solution)/shard_map/concatenate | solution.py:64
  12.7 2.8 %fusion.36 = f32[2,8,128,128]{3,2,1,0:T(8,128)} fusion(f32[2,640,128,8]{2,1,3,0:T(8,128)S(1)} %get-tuple-element.372, f32[2,8,128]{2,1,0:T(8,128)S(1)} %broadcast_maximum_fusion, pred[128,640]{0,1:T(8,128)(4,1)S(1)} %compare_select_fusion.1, f32[2,8,128]{2,1,0:T(8,128)S(1)} %get-tuple-element.369, bf16[128,2,128]{2,0,1:T(8,128)(2,1)S(1)} %get-tuple-element.365, ...), kind=kOutput, calls=%fused_computation.46 | convolution fusion | flops 343015424 | bytes 6717440 | tf_op jit(solution)/shard_map/hgtl,lhd->hgtd/dot_general | solution.py:97
  15.5 67.8 %while.25 = (s32[]{:T(128)}, f32[2,8,128]{2,1,0:T(8,128)S(1)}, f32[2,8,128]{2,1,0:T(8,128)S(1)}, f32[2,8,128,128]{3,2,1,0:T(8,128)}, bf16[640,2,128]{2,0,1:T(8,1...) while((s32[]{:T(128)}, f32[2,8,128]{2,1,0:T(8,128)S(1)}, ...), condition=%wide.region_7.8_spmd.clone, body=%wide.region_3.7_spmd.clone.sunk | while | flops 688849152 | bytes 31804344 | solution.py:125
  15.5 2.5 %collective-permute-start = (bf16[640,2,128]{2,0,1:T(8,128)(2,1)}, bf16[640,2,128]{2,0,1:T(8,128)(2,1)S(1)}, u32[]{:S(2)}, u32[]{:S(2)}) collective-permute-start(bf16[640,2,128]{2,0,1:T(8,128)(2,1)} %get-tuple-element.469), channel_id=1, source_target_pairs={{0,4},{4,8},{8,12},{12,0},{1,5},{5,9},{9,13},{13,1},{2,6},{6,10},{... | collective-permute-start | bytes 983048 | tf_op jit(solution)/shard_map/while/body/eval_jaxpr/ppermute | solution.py:15
  18.0 1.6 %collective-permute-start.1 = (bf16[640,2,128]{2,0,1:T(8,128)(2,1)}, bf16[640,2,128]{2,0,1:T(8,128)(2,1)S(1)}, u32[]{:S(2)}, u32[]{:S(2)}) collective-permute-start(bf16[640,2,128]{2,0,1:T(8,128)(2,1)} %get-tuple-element.470), channel_id=1, source_target_pairs={{0,4},{4,8},{8,12},{12,0},{1,5},{5,9},{9,13},{13,1},{2,6},{6,10},{... | collective-permute-start | bytes 983048 | tf_op jit(solution)/shard_map/while/body/eval_jaxpr/ppermute | solution.py:15
  19.6 0.1 select_reduce_fusion.3
  19.7 0.3 compare_select_fusion.3
  20.0 8.7 %collective-permute-done = bf16[640,2,128]{2,0,1:T(8,128)(2,1)S(1)} collective-permute-done((bf16[640,2,128]{2,0,1:T(8,128)(2,1)}, bf16[640,2,128]{2,0,1:T(8,128)(2,1)S(1)}, u32[]{:S(2)}, u32[]{:S(2)}) %collective-permute-start) | collective-permute-done | bytes 327712 | tf_op jit(solution)/shard_map/while/body/eval_jaxpr/ppermute | solution.py:15
  28.8 0.9 %fusion.85 = (f32[2,8,128]{2,1,0:T(8,128)S(1)}, f32[2,640,128,8]{2,1,3,0:T(8,128)S(1)}) fusion(pred[128,640]{0,1:T(8,128)(4,1)S(1)} %compare_select_fusion.3, bf16[128,2,8,128]{3,0,2,1:T(8,128)(2,1)S(1)} %get-tuple-element.488, bf16[640,2,128]{2,0,1:T(8,128)(2,1)S(1)} %collective-permute-done), kind=kOutput, calls=%fused_computation.4.clone.1 | convolution fusion | flops 339474432 | bytes 6184960 | tf_op jit(solution)/shard_map/while/body/eval_jaxpr/thgd,lhd->hgtl/dot_general | solution.py:89
  29.7 1.2 %fusion.86 = f32[2,8,128]{2,1,0:T(8,128)S(1)} fusion(f32[2,640,128,8]{2,1,3,0:T(8,128)S(1)} %get-tuple-element.447, f32[2,8,128]{2,1,0:T(8,128)S(1)} %max.13, pred[128,640]{0,1:T(8,128)(4,1)S(1)} %compare_select_fusion.3), kind=kLoop, calls=%fused_computation.6.clone.1 | loop fusion | flops 6551552 | bytes 5341184 | tf_op jit(solution)/shard_map/while/body/eval_jaxpr/reduce_sum | solution.py:96
  31.0 0.7 copy.74
  31.7 3.9 %collective-permute-done.1 = bf16[640,2,128]{2,0,1:T(8,128)(2,1)S(1)} collective-permute-done((bf16[640,2,128]{2,0,1:T(8,128)(2,1)}, bf16[640,2,128]{2,0,1:T(8,128)(2,1)S(1)}, u32[]{:S(2)}, u32[]{:S(2)}) %collective-permute-start.1) | collective-permute-done | bytes 327712 | tf_op jit(solution)/shard_map/while/body/eval_jaxpr/ppermute | solution.py:15
  35.6 0.7 copy.75
  36.3 0.0 copy-done.1
  36.3 2.1 %fusion.87 = f32[2,8,128,128]{3,2,1,0:T(8,128)S(1)} fusion(f32[2,640,128,8]{2,1,3,0:T(8,128)S(1)} %get-tuple-element.447, f32[2,8,128]{2,1,0:T(8,128)S(1)} %max.13, pred[128,640]{0,1:T(8,128)(4,1)S(1)} %compare_select_fusion.3, f32[2,8,128,128]{3,2,1,0:T(8,128)S(1)} %copy-done.1, f32[2,8,128]{2,1,0:T(8,128)S(1)} %get-tuple-element.449, ...), kind=kOutput, calls=%fused_computation.9.clone.1 | convolution fusion | flops 342622208 | bytes 7766016 | tf_op jit(solution)/shard_map/while/body/eval_jaxpr/hgtl,lhd->hgtd/dot_general | solution.py:97
  38.4 1.0 %copy-done.2 = f32[2,8,128,128]{3,2,1,0:T(8,128)} copy-done((f32[2,8,128,128]{3,2,1,0:T(8,128)}, f32[2,8,128,128]{3,2,1,0:T(8,128)S(1)}, u32[]{:S(2)}) %copy-start.2) | copy-done | bytes 1048600 | tf_op jit(solution)/shard_map/while
  39.4 0.0 collective-permute-start
  39.4 1.3 %collective-permute-start.1 = (bf16[640,2,128]{2,0,1:T(8,128)(2,1)}, bf16[640,2,128]{2,0,1:T(8,128)(2,1)S(1)}, u32[]{:S(2)}, u32[]{:S(2)}) collective-permute-start(bf16[640,2,128]{2,0,1:T(8,128)(2,1)} %get-tuple-element.470), channel_id=1, source_target_pairs={{0,4},{4,8},{8,12},{12,0},{1,5},{5,9},{9,13},{13,1},{2,6},{6,10},{... | collective-permute-start | bytes 983048 | tf_op jit(solution)/shard_map/while/body/eval_jaxpr/ppermute | solution.py:15
  40.7 0.1 select_reduce_fusion.3
  40.8 0.3 compare_select_fusion.3
  41.2 10.8 %collective-permute-done = bf16[640,2,128]{2,0,1:T(8,128)(2,1)S(1)} collective-permute-done((bf16[640,2,128]{2,0,1:T(8,128)(2,1)}, bf16[640,2,128]{2,0,1:T(8,128)(2,1)S(1)}, u32[]{:S(2)}, u32[]{:S(2)}) %collective-permute-start) | collective-permute-done | bytes 327712 | tf_op jit(solution)/shard_map/while/body/eval_jaxpr/ppermute | solution.py:15
  52.0 0.9 %fusion.85 = (f32[2,8,128]{2,1,0:T(8,128)S(1)}, f32[2,640,128,8]{2,1,3,0:T(8,128)S(1)}) fusion(pred[128,640]{0,1:T(8,128)(4,1)S(1)} %compare_select_fusion.3, bf16[128,2,8,128]{3,0,2,1:T(8,128)(2,1)S(1)} %get-tuple-element.488, bf16[640,2,128]{2,0,1:T(8,128)(2,1)S(1)} %collective-permute-done), kind=kOutput, calls=%fused_computation.4.clone.1 | convolution fusion | flops 339474432 | bytes 6184960 | tf_op jit(solution)/shard_map/while/body/eval_jaxpr/thgd,lhd->hgtl/dot_general | solution.py:89
  52.9 1.2 %fusion.86 = f32[2,8,128]{2,1,0:T(8,128)S(1)} fusion(f32[2,640,128,8]{2,1,3,0:T(8,128)S(1)} %get-tuple-element.447, f32[2,8,128]{2,1,0:T(8,128)S(1)} %max.13, pred[128,640]{0,1:T(8,128)(4,1)S(1)} %compare_select_fusion.3), kind=kLoop, calls=%fused_computation.6.clone.1 | loop fusion | flops 6551552 | bytes 5341184 | tf_op jit(solution)/shard_map/while/body/eval_jaxpr/reduce_sum | solution.py:96
  54.2 0.7 copy.74
  54.9 3.1 %collective-permute-done.1 = bf16[640,2,128]{2,0,1:T(8,128)(2,1)S(1)} collective-permute-done((bf16[640,2,128]{2,0,1:T(8,128)(2,1)}, bf16[640,2,128]{2,0,1:T(8,128)(2,1)S(1)}, u32[]{:S(2)}, u32[]{:S(2)}) %collective-permute-start.1) | collective-permute-done | bytes 327712 | tf_op jit(solution)/shard_map/while/body/eval_jaxpr/ppermute | solution.py:15
  58.0 0.7 copy.75
  58.7 2.1 %fusion.87 = f32[2,8,128,128]{3,2,1,0:T(8,128)S(1)} fusion(f32[2,640,128,8]{2,1,3,0:T(8,128)S(1)} %get-tuple-element.447, f32[2,8,128]{2,1,0:T(8,128)S(1)} %max.13, pred[128,640]{0,1:T(8,128)(4,1)S(1)} %compare_select_fusion.3, f32[2,8,128,128]{3,2,1,0:T(8,128)S(1)} %copy-done.1, f32[2,8,128]{2,1,0:T(8,128)S(1)} %get-tuple-element.449, ...), kind=kOutput, calls=%fused_computation.9.clone.1 | convolution fusion | flops 342622208 | bytes 7766016 | tf_op jit(solution)/shard_map/while/body/eval_jaxpr/hgtl,lhd->hgtd/dot_general | solution.py:97
  60.8 1.0 %copy-done.2 = f32[2,8,128,128]{3,2,1,0:T(8,128)} copy-done((f32[2,8,128,128]{3,2,1,0:T(8,128)}, f32[2,8,128,128]{3,2,1,0:T(8,128)S(1)}, u32[]{:S(2)}) %copy-start.2) | copy-done | bytes 1048600 | tf_op jit(solution)/shard_map/while
  61.8 0.0 collective-permute-start
  61.8 0.0 collective-permute-start.1
  61.8 0.1 select_reduce_fusion.3
  61.9 0.3 compare_select_fusion.3
  62.2 12.2 %collective-permute-done = bf16[640,2,128]{2,0,1:T(8,128)(2,1)S(1)} collective-permute-done((bf16[640,2,128]{2,0,1:T(8,128)(2,1)}, bf16[640,2,128]{2,0,1:T(8,128)(2,1)S(1)}, u32[]{:S(2)}, u32[]{:S(2)}) %collective-permute-start) | collective-permute-done | bytes 327712 | tf_op jit(solution)/shard_map/while/body/eval_jaxpr/ppermute | solution.py:15
  74.4 0.9 %fusion.85 = (f32[2,8,128]{2,1,0:T(8,128)S(1)}, f32[2,640,128,8]{2,1,3,0:T(8,128)S(1)}) fusion(pred[128,640]{0,1:T(8,128)(4,1)S(1)} %compare_select_fusion.3, bf16[128,2,8,128]{3,0,2,1:T(8,128)(2,1)S(1)} %get-tuple-element.488, bf16[640,2,128]{2,0,1:T(8,128)(2,1)S(1)} %collective-permute-done), kind=kOutput, calls=%fused_computation.4.clone.1 | convolution fusion | flops 339474432 | bytes 6184960 | tf_op jit(solution)/shard_map/while/body/eval_jaxpr/thgd,lhd->hgtl/dot_general | solution.py:89
  75.3 1.2 %fusion.86 = f32[2,8,128]{2,1,0:T(8,128)S(1)} fusion(f32[2,640,128,8]{2,1,3,0:T(8,128)S(1)} %get-tuple-element.447, f32[2,8,128]{2,1,0:T(8,128)S(1)} %max.13, pred[128,640]{0,1:T(8,128)(4,1)S(1)} %compare_select_fusion.3), kind=kLoop, calls=%fused_computation.6.clone.1 | loop fusion | flops 6551552 | bytes 5341184 | tf_op jit(solution)/shard_map/while/body/eval_jaxpr/reduce_sum | solution.py:96
  76.6 0.7 copy.74
  77.3 2.1 %collective-permute-done.1 = bf16[640,2,128]{2,0,1:T(8,128)(2,1)S(1)} collective-permute-done((bf16[640,2,128]{2,0,1:T(8,128)(2,1)}, bf16[640,2,128]{2,0,1:T(8,128)(2,1)S(1)}, u32[]{:S(2)}, u32[]{:S(2)}) %collective-permute-start.1) | collective-permute-done | bytes 327712 | tf_op jit(solution)/shard_map/while/body/eval_jaxpr/ppermute | solution.py:15
  79.4 0.7 copy.75
  80.2 0.0 copy-done.1
  80.2 2.1 %fusion.87 = f32[2,8,128,128]{3,2,1,0:T(8,128)S(1)} fusion(f32[2,640,128,8]{2,1,3,0:T(8,128)S(1)} %get-tuple-element.447, f32[2,8,128]{2,1,0:T(8,128)S(1)} %max.13, pred[128,640]{0,1:T(8,128)(4,1)S(1)} %compare_select_fusion.3, f32[2,8,128,128]{3,2,1,0:T(8,128)S(1)} %copy-done.1, f32[2,8,128]{2,1,0:T(8,128)S(1)} %get-tuple-element.449, ...), kind=kOutput, calls=%fused_computation.9.clone.1 | convolution fusion | flops 342622208 | bytes 7766016 | tf_op jit(solution)/shard_map/while/body/eval_jaxpr/hgtl,lhd->hgtd/dot_general | solution.py:97
  82.3 0.0 copy-start.2
  82.3 1.0 %copy-done.2 = f32[2,8,128,128]{3,2,1,0:T(8,128)} copy-done((f32[2,8,128,128]{3,2,1,0:T(8,128)}, f32[2,8,128,128]{3,2,1,0:T(8,128)S(1)}, u32[]{:S(2)}) %copy-start.2) | copy-done | bytes 1048600 | tf_op jit(solution)/shard_map/while
  83.2 0.1 copy.31
  83.4 2.7 %fusion.50 = bf16[128,2,8,128]{3,2,1,0:T(8,128)(2,1)} fusion(f32[2,8,128]{1,0,2:T(2,128)S(1)} %copy.31, f32[2,8,128,128]{3,2,1,0:T(8,128)} %get-tuple-element.313), kind=kLoop, calls=%fused_computation.56 | loop fusion | flops 524288 | bytes 1581056 | tf_op jit(solution)/shard_map/convert_element_type | solution.py:130
  (41 shorter events, 0.3 us)
Async XLA Ops:
  0.0 4.6 %copy-start = (bf16[128,8192]{1,0:T(8,128)(2,1)S(1)}, bf16[128,8192]{1,0:T(8,128)(2,1)}, u32[]{:S(2)}) copy-start(bf16[128,8192]{1,0:T(8,128)(2,1)} %param.12) | copy-start | bytes 6291460
  0.0 9.1 %copy-start.6 = (bf16[4,16,2,2,128]{4,3,2,1,0:T(2,128)(2,1)S(1)}, bf16[4,16,2,2,128]{4,3,2,1,0:T(2,128)(2,1)}, u32[]{:S(2)}) copy-start(bf16[4,16,2,2,128]{4,3,2,1,0:T(2,128)(2,1)} %param.15) | copy-start | bytes 196612
  0.0 9.1 %copy-start.5 = (bf16[128,2,2,128]{3,2,1,0:T(2,128)(2,1)S(1)}, bf16[128,2,2,128]{3,2,1,0:T(2,128)(2,1)}, u32[]{:S(2)}) copy-start(bf16[128,2,2,128]{3,2,1,0:T(2,128)(2,1)} %param.17) | copy-start | bytes 393220
  0.0 9.3 %copy-start.4 = (bf16[4,16,2,8,128]{4,3,2,1,0:T(8,128)(2,1)S(1)}, bf16[4,16,2,8,128]{4,3,2,1,0:T(8,128)(2,1)}, u32[]{:S(2)}) copy-start(bf16[4,16,2,8,128]{4,3,2,1,0:T(8,128)(2,1)} %param.14) | copy-start | bytes 786436
  0.0 9.3 %copy-start.3 = (bf16[128,2,8,128]{3,2,1,0:T(8,128)(2,1)S(1)}, bf16[128,2,8,128]{3,2,1,0:T(8,128)(2,1)}, u32[]{:S(2)}) copy-start(bf16[128,2,8,128]{3,2,1,0:T(8,128)(2,1)} %param.16) | copy-start | bytes 1572868
  0.0 6.8 %collective-permute-start.2 = (bf16[2,8192,48]{1,2,0:T(8,128)(2,1)}, bf16[2,8192,48]{1,2,0:T(8,128)(2,1)}, u32[]{:S(2)}, u32[]{:S(2)}) collective-permute-start(bf16[2,8192,48]{1,2,0:T(8,128)(2,1)} %param.13), channel_id=1, source_target_pairs={{0,1},{1,0},{2,3},{3,2},{4,5},{5,4},{6,7},{7,6},{8,9},{9,8},{10,11... | collective-permute-start | bytes 4718600 | tf_op jit(solution)/shard_map/ppermute | solution.py:10
  12.7 2.8 %copy-start.7 = (s32[4]{0:T(128)S(1)}, s32[4]{0:T(128)}, u32[]{:S(2)}) copy-start(s32[4]{0:T(128)} %param.21) | copy-start | bytes 52
  15.5 13.3 %collective-permute-start = (bf16[640,2,128]{2,0,1:T(8,128)(2,1)}, bf16[640,2,128]{2,0,1:T(8,128)(2,1)S(1)}, u32[]{:S(2)}, u32[]{:S(2)}) collective-permute-start(bf16[640,2,128]{2,0,1:T(8,128)(2,1)} %get-tuple-element.469), channel_id=1, source_target_pairs={{0,4},{4,8},{8,12},{12,0},{1,5},{5,9},{9,13},{13,1},{2,6},{6,10},{... | collective-permute-start | bytes 983048 | tf_op jit(solution)/shard_map/while/body/eval_jaxpr/ppermute | solution.py:15
  18.0 17.6 %collective-permute-start.1 = (bf16[640,2,128]{2,0,1:T(8,128)(2,1)}, bf16[640,2,128]{2,0,1:T(8,128)(2,1)S(1)}, u32[]{:S(2)}, u32[]{:S(2)}) collective-permute-start(bf16[640,2,128]{2,0,1:T(8,128)(2,1)} %get-tuple-element.470), channel_id=1, source_target_pairs={{0,4},{4,8},{8,12},{12,0},{1,5},{5,9},{9,13},{13,1},{2,6},{6,10},{... | collective-permute-start | bytes 983048 | tf_op jit(solution)/shard_map/while/body/eval_jaxpr/ppermute | solution.py:15
  28.8 7.5 %copy-start.1 = (f32[2,8,128,128]{3,2,1,0:T(8,128)S(1)}, f32[2,8,128,128]{3,2,1,0:T(8,128)}, u32[]{:S(2)}) copy-start(f32[2,8,128,128]{3,2,1,0:T(8,128)} %get-tuple-element.468) | copy-start | bytes 3145732 | tf_op jit(solution)/shard_map/while
  38.4 1.0 %copy-start.2 = (f32[2,8,128,128]{3,2,1,0:T(8,128)}, f32[2,8,128,128]{3,2,1,0:T(8,128)S(1)}, u32[]{:S(2)}) copy-start(f32[2,8,128,128]{3,2,1,0:T(8,128)S(1)} %fusion.87) | copy-start | bytes 3145732 | tf_op jit(solution)/shard_map/while
  39.4 12.6 %collective-permute-start = (bf16[640,2,128]{2,0,1:T(8,128)(2,1)}, bf16[640,2,128]{2,0,1:T(8,128)(2,1)S(1)}, u32[]{:S(2)}, u32[]{:S(2)}) collective-permute-start(bf16[640,2,128]{2,0,1:T(8,128)(2,1)} %get-tuple-element.469), channel_id=1, source_target_pairs={{0,4},{4,8},{8,12},{12,0},{1,5},{5,9},{9,13},{13,1},{2,6},{6,10},{... | collective-permute-start | bytes 983048 | tf_op jit(solution)/shard_map/while/body/eval_jaxpr/ppermute | solution.py:15
  39.4 18.5 %collective-permute-start.1 = (bf16[640,2,128]{2,0,1:T(8,128)(2,1)}, bf16[640,2,128]{2,0,1:T(8,128)(2,1)S(1)}, u32[]{:S(2)}, u32[]{:S(2)}) collective-permute-start(bf16[640,2,128]{2,0,1:T(8,128)(2,1)} %get-tuple-element.470), channel_id=1, source_target_pairs={{0,4},{4,8},{8,12},{12,0},{1,5},{5,9},{9,13},{13,1},{2,6},{6,10},{... | collective-permute-start | bytes 983048 | tf_op jit(solution)/shard_map/while/body/eval_jaxpr/ppermute | solution.py:15
  52.0 6.7 %copy-start.1 = (f32[2,8,128,128]{3,2,1,0:T(8,128)S(1)}, f32[2,8,128,128]{3,2,1,0:T(8,128)}, u32[]{:S(2)}) copy-start(f32[2,8,128,128]{3,2,1,0:T(8,128)} %get-tuple-element.468) | copy-start | bytes 3145732 | tf_op jit(solution)/shard_map/while
  60.8 1.0 %copy-start.2 = (f32[2,8,128,128]{3,2,1,0:T(8,128)}, f32[2,8,128,128]{3,2,1,0:T(8,128)S(1)}, u32[]{:S(2)}) copy-start(f32[2,8,128,128]{3,2,1,0:T(8,128)S(1)} %fusion.87) | copy-start | bytes 3145732 | tf_op jit(solution)/shard_map/while
  61.8 12.7 %collective-permute-start = (bf16[640,2,128]{2,0,1:T(8,128)(2,1)}, bf16[640,2,128]{2,0,1:T(8,128)(2,1)S(1)}, u32[]{:S(2)}, u32[]{:S(2)}) collective-permute-start(bf16[640,2,128]{2,0,1:T(8,128)(2,1)} %get-tuple-element.469), channel_id=1, source_target_pairs={{0,4},{4,8},{8,12},{12,0},{1,5},{5,9},{9,13},{13,1},{2,6},{6,10},{... | collective-permute-start | bytes 983048 | tf_op jit(solution)/shard_map/while/body/eval_jaxpr/ppermute | solution.py:15
  61.8 17.7 %collective-permute-start.1 = (bf16[640,2,128]{2,0,1:T(8,128)(2,1)}, bf16[640,2,128]{2,0,1:T(8,128)(2,1)S(1)}, u32[]{:S(2)}, u32[]{:S(2)}) collective-permute-start(bf16[640,2,128]{2,0,1:T(8,128)(2,1)} %get-tuple-element.470), channel_id=1, source_target_pairs={{0,4},{4,8},{8,12},{12,0},{1,5},{5,9},{9,13},{13,1},{2,6},{6,10},{... | collective-permute-start | bytes 983048 | tf_op jit(solution)/shard_map/while/body/eval_jaxpr/ppermute | solution.py:15
  74.4 5.8 %copy-start.1 = (f32[2,8,128,128]{3,2,1,0:T(8,128)S(1)}, f32[2,8,128,128]{3,2,1,0:T(8,128)}, u32[]{:S(2)}) copy-start(f32[2,8,128,128]{3,2,1,0:T(8,128)} %get-tuple-element.468) | copy-start | bytes 3145732 | tf_op jit(solution)/shard_map/while
  82.3 1.0 %copy-start.2 = (f32[2,8,128,128]{3,2,1,0:T(8,128)}, f32[2,8,128,128]{3,2,1,0:T(8,128)S(1)}, u32[]{:S(2)}) copy-start(f32[2,8,128,128]{3,2,1,0:T(8,128)S(1)} %fusion.87) | copy-start | bytes 3145732 | tf_op jit(solution)/shard_map/while
where the time goes:
time: 86.4 us; the launch traced here: 86.1 us
  waiting for transfers between devices  40.8 us (47%)
  matrix products  17.5 us (20%)
  other arithmetic  11.8 us (14%)
  local copies, waits for them, and re-layouts  9.65 us (11%)
  starting transfers between devices  5.9 us (7%)
    ppermute x6, waiting for transfers between devices, from_behind(): lax.ppermute(value, axis, [(i, (i + by) % devices) for i in range(devices)])  40.8 us
    dot_general x4, matrix products, attend(): jnp.einsum('hgtl,lhd->hgtd', weights.astype(jnp.bfloat16), value_block, p...  9.07 us
    while x21, local copies, waits for them, and re-layouts  7.24 us
    ppermute x6, starting transfers between devices, from_behind(): lax.ppermute(value, axis, [(i, (i + by) % devices) for i in range(devices)])  5.37 us
    reduce_sum x4, other arithmetic, attend(): running_sum = running_sum * factor + jnp.sum(weights, axis=-1)  5 us
    dot_general x4, matrix products, attend(): jnp.einsum('thgd,lhd->hgtl', query_rows, key_block, preferred_element_typ...  3.48 us
    convert_element_type x1, other arithmetic, per_device(): return jnp.transpose(output, (2, 0, 1, 3)).astype(jnp.bfloat16)  2.72 us
    unnamed x14, local copies, waits for them, and re-layouts  2.26 us
  transfers between devices with their start and end apart: 7, of which 6 were waited for; matrix products, arithmetic and copies ran while one was open for 19% of the time, Pallas kernels for 0%

commit v1 on v0

v1 whole, which is shorter than its diff:
```python
import functools

import jax
import jax.numpy as jnp
from jax import lax
from jax.experimental import pallas as pl
from jax.experimental.pallas import tpu as pltpu
from jax.sharding import PartitionSpec as P

FILL = -1e30
MESH = pl.DeviceIdType.MESH
TILE = 256
F32 = jnp.float32
BF16 = jnp.bfloat16


def iota(shape, dim):
    return lax.broadcasted_iota(jnp.int32, shape, dim)


def dot(a, b, ca=1, cb=0):
    return lax.dot_general(a, b, (((ca,), (cb,)), ((), ())), preferred_element_type=F32)


def kernel(
    n, heads, groups, slots, rank,
    tok_hbm, down_hbm, aq_ref, akv_ref, qb_ref, kvb_ref, ck_hbm, cv_hbm, slot_ref, len_ref,
    out_ref,
    tok_v, down_v, raw, kv, q, acc, top, total, xch, local_sem,
    send_rc, recv_rc, send_rf, recv_rf, send_lc, recv_lc, send_x, recv_x,
):
    me = lax.axis_index("ctx")
    rep = lax.axis_index("rep")
    toks = tok_v.shape[0]
    cached = ck_hbm.shape[0] // heads
    rows_all = cached + toks
    width = 3 * rank
    own_slots = down_hbm.shape[0] // width
    hd = q.shape[2]
    q_rows = toks * groups

    load_k = pltpu.make_async_copy(ck_hbm, raw.at[0], local_sem.at[0])
    load_v = pltpu.make_async_copy(cv_hbm, raw.at[1], local_sem.at[1])
    load_t = pltpu.make_async_copy(tok_hbm, tok_v, local_sem.at[2])
    load_d = pltpu.make_async_copy(down_hbm, down_v, local_sem.at[3])
    for load in (load_k, load_v, load_t, load_d):
        load.start()

    barrier = pltpu.get_barrier_semaphore()
    pl.semaphore_signal(barrier, inc=1, device_id={"rep": 1 - rep}, device_id_type=MESH)

    @pl.when(me > 0)
    def _():
        pl.semaphore_signal(barrier, inc=1, device_id={"ctx": me - 1}, device_id_type=MESH)

    @pl.when(me < n - 1)
    def _():
        pl.semaphore_signal(barrier, inc=1, device_id={"ctx": me + 1}, device_id_type=MESH)

    neighbours = 1 + jnp.where(me > 0, 1, 0) + jnp.where(me < n - 1, 1, 0)

    def cached_right(src):
        part = kv.at[src, :, :, pl.ds(0, cached)]
        return pltpu.make_async_remote_copy(
            src_ref=part, dst_ref=part, send_sem=send_rc.at[src], recv_sem=recv_rc.at[src],
            device_id={"ctx": me + 1}, device_id_type=MESH)

    def fresh_right(src):
        part = kv.at[src, :, :, pl.ds(cached, toks)]
        return pltpu.make_async_remote_copy(
            src_ref=part, dst_ref=part, send_sem=send_rf.at[src], recv_sem=recv_rf.at[src],
            device_id={"ctx": me + 1}, device_id_type=MESH)

    def cached_left(src):
        part = kv.at[src, :, :, pl.ds(0, cached)]
        return pltpu.make_async_remote_copy(
            src_ref=part, dst_ref=part, send_sem=send_lc.at[src], recv_sem=recv_lc.at[src],
            device_id={"ctx": me - 1}, device_id_type=MESH)

    step = 128
    load_k.wait()
    load_v.wait()
    for h in range(heads):
        pick = (iota((step, step * heads), 1) == iota((step, step * heads), 0) * heads + h)
        pick = pick.astype(F32).astype(BF16)
        for c in range(2):
            for b in range(cached // step):
                block = raw[c, pl.ds(b * step * heads, step * heads), :]
                kv[me, h, c, pl.ds(b * step, step), :] = dot(pick, block).astype(BF16)

    pl.semaphore_wait(barrier, neighbours)

    @pl.when(me < n - 1)
    def _():
        cached_right(me).start()

    @pl.when(me > 0)
    def _():
        cached_left(me).start()

    load_t.wait()
    load_d.wait()
    slot = slot_ref[...]
    own = dot(down_v[...], tok_v[...], 1, 1).astype(BF16).astype(F32)
    part = jnp.zeros((width, toks), F32)
    for k in range(own_slots):
        part = part + jnp.where(slot == rep * own_slots + k, own[k * width:(k + 1) * width], 0.0)
    xch[0] = part
    swap = pltpu.make_async_remote_copy(
        src_ref=xch.at[0], dst_ref=xch.at[1], send_sem=send_x, recv_sem=recv_x,
        device_id={"rep": 1 - rep}, device_id_type=MESH)
    swap.start()
    swap.wait_recv()
    shrunk = part + xch[1]

    def spread(rows):
        return jnp.concatenate(
            [jnp.where(slot == s, rows, 0.0) for s in range(slots)], axis=0).astype(BF16)

    def expand(cols_each):
        shape = (slots * rank, slots * rank * cols_each)
        first = iota(shape, 0) * cols_each
        col = iota(shape, 1)
        return ((col >= first) & (col < first + cols_each)).astype(F32).astype(BF16)

    akv = akv_ref[...]
    kvb = kvb_ref[...]
    each = 2 * heads
    for c in range(2):
        wide = dot(spread(shrunk[rank * (1 + c):rank * (2 + c)]), expand(each), 0, 0)
        for h in range(heads):
            keep = lax.rem(iota(wide.shape, 1), each) == c * heads + h
            delta = dot(jnp.where(keep, wide, 0.0).astype(BF16), akv)
            shape = (toks, toks * each)
            pick = (iota(shape, 1) == iota(shape, 0) * each + c * heads + h)
            base = dot(pick.astype(F32).astype(BF16), kvb)
            kv[me, h, c, pl.ds(cached, toks), :] = (base + delta).astype(BF16)

    @pl.when(me < n - 1)
    def _():
        fresh_right(me).start()

    each = heads * groups
    wide = dot(spread(shrunk[0:rank]), expand(each), 0, 0)
    wide = jnp.broadcast_to(wide[:, None, :], (toks, groups, wide.shape[1]))
    wide = wide.reshape(q_rows, wide.shape[2])
    aq = aq_ref[...]
    base_all = qb_ref[...].astype(F32).reshape(toks, each, hd)
    for h in range(heads):
        keep = lax.rem(iota(wide.shape, 1), each) == h * groups + lax.rem(iota(wide.shape, 0), groups)
        delta = dot(jnp.where(keep, wide, 0.0).astype(BF16), aq)
        base = base_all[:, h * groups:(h + 1) * groups].reshape(q_rows, hd)
        q[h] = (base + delta).astype(BF16)

    top[...] = jnp.full(top.shape, FILL, F32)
    total[...] = jnp.zeros(total.shape, F32)
    acc[...] = jnp.zeros(acc.shape, F32)
    tiles = q_rows // TILE
    scale = hd ** -0.5

    def process(src, rows, causal):
        limit = len_ref[src]

        def body(index, carry):
            h = index // tiles
            j = index % tiles
            cols = pl.ds(pl.multiple_of(j * TILE, TILE), TILE)
            scores = dot(kv[src, h, 0, pl.ds(0, rows), :], q[h, cols, :], 1, 1) * scale
            row = iota(scores.shape, 0)
            seen = row < limit
            if rows > cached:
                if causal:
                    token = lax.div(j * TILE + iota(scores.shape, 1), groups)
                    seen = seen & (row < cached) | (row >= cached) & (row - cached <= token)
                else:
                    seen = seen | (row >= cached)
            scores = jnp.where(seen, scores, FILL)
            old = top[h, :, cols]
            new = jnp.maximum(old, jnp.max(scores, axis=0, keepdims=True))
            weights = jnp.exp(scores - new)
            factor = jnp.exp(old - new)
            top[h, :, cols] = new
            total[h, :, cols] = total[h, :, cols] * factor + jnp.sum(weights, axis=0, keepdims=True)
            acc[h, :, cols] = acc[h, :, cols] * factor + dot(
                kv[src, h, 1, pl.ds(0, rows), :], weights.astype(BF16), 0, 0)
            return carry

        lax.fori_loop(0, heads * tiles, body, 0)

    process(me, rows_all, True)

    def arrive(t, carry):
        @pl.when(me - t >= 0)
        def _():
            cached_right(me - t).wait_recv()

            @pl.when(me < n - 1)
            def _():
                cached_right(me - t).start()

            fresh_right(me - t).wait_recv()

            @pl.when(me < n - 1)
            def _():
                fresh_right(me - t).start()

        @pl.when(me + t < n)
        def _():
            cached_left(me + t).wait_recv()

            @pl.when(me > 0)
            def _():
                cached_left(me + t).start()

        @pl.when(me - t >= 0)
        def _():
            process(me - t, rows_all, False)

        @pl.when(me + t < n)
        def _():
            process(me + t, cached, False)

        return carry

    lax.fori_loop(1, n, arrive, 0)

    results = []
    for h in range(heads):
        result = (acc[h] / total[h]).T
        results.append(result.reshape(toks, groups, hd))
    result = jnp.concatenate(results, axis=1) if heads > 1 else results[0]
    out_ref[...] = result.reshape(toks * heads * groups, hd).astype(BF16)

    swap.wait_send()

    def drain(t, carry):
        @pl.when((me - t >= 0) & (me < n - 1))
        def _():
            cached_right(me - t).wait_send()
            fresh_right(me - t).wait_send()

        @pl.when((me + t < n) & (me > 0))
        def _():
            cached_left(me + t).wait_send()

        return carry

    lax.fori_loop(0, n, drain, 0)


def per_device(
    tokens, adapter_down, adapter_query, adapter_keyvalue, query_base, keyvalue_base,
    cached_keys, cached_values, adapter_slot, cached_length,
):
    n = cached_length.shape[0]
    toks, depth = tokens.shape
    slots, rank, heads, groups, hd = adapter_query.shape
    cached = cached_keys.shape[0]
    down = jnp.swapaxes(adapter_down, 1, 2).reshape(-1, depth)
    vmem = pl.BlockSpec(memory_space=pltpu.VMEM)
    hbm = pl.BlockSpec(memory_space=pl.ANY)
    smem = pl.BlockSpec(memory_space=pltpu.SMEM)
    dma = pltpu.SemaphoreType.DMA
    q_rows = toks * groups
    out = pl.pallas_call(
        functools.partial(kernel, n, heads, groups, slots, rank),
        out_shape=jax.ShapeDtypeStruct((toks * heads * groups, hd), BF16),
        in_specs=[hbm, hbm, vmem, vmem, vmem, vmem, hbm, hbm, vmem, smem],
        out_specs=vmem,
        scratch_shapes=[
            pltpu.VMEM((toks, depth), BF16),
            pltpu.VMEM(down.shape, BF16),
            pltpu.VMEM((2, cached * heads, hd), BF16),
            pltpu.VMEM((n, heads, 2, cached + toks, hd), BF16),
            pltpu.VMEM((heads, q_rows, hd), BF16),
            pltpu.VMEM((heads, hd, q_rows), F32),
            pltpu.VMEM((heads, 1, q_rows), F32),
            pltpu.VMEM((heads, 1, q_rows), F32),
            pltpu.VMEM((2, 3 * rank, toks), F32),
            dma((4,)),
            dma((n,)), dma((n,)), dma((n,)), dma((n,)), dma((n,)), dma((n,)), dma, dma,
        ],
        compiler_params=pltpu.CompilerParams(
            collective_id=0, has_side_effects=True, vmem_limit_bytes=48 * 1024 * 1024),
    )(
        tokens, down,
        adapter_query.reshape(-1, hd), adapter_keyvalue.reshape(-1, hd),
        query_base.reshape(-1, hd), keyvalue_base.reshape(-1, hd),
        cached_keys.reshape(-1, hd), cached_values.reshape(-1, hd),
        adapter_slot, cached_length,
    )
    return out.reshape(toks, heads, groups, hd)


def solution(mesh):
    in_specs = (
        P(("group", "ctx"), None),
        P(("group", "ctx", "rep"), None, None),
        P(("group", "ctx"), None, ("tp", "rep"), None, None),
        P(("group", "ctx"), None, None, ("tp", "rep"), None),
        P(("group", "ctx"), ("tp", "rep"), None, None),
        P(("group", "ctx"), None, ("tp", "rep"), None),
        P(("group", "ctx"), ("tp", "rep"), None),
        P(("group", "ctx"), ("tp", "rep"), None),
        P(("group", "ctx"), None),
        P("group"),
    )
    out_specs = P(("group", "ctx"), ("tp", "rep"), None, None)
    return jax.shard_map(
        per_device, mesh=mesh, in_specs=in_specs, out_specs=out_specs, check_vma=False
    )
```

time: 86.4 us -> 62.1 us (0.72)
  the two profiles are of different devices: /device:TPU:0 before, /device:TPU:30 now
where the time goes in v1:
time: 62.1 us; the launch traced here: 61.7 us
  Pallas kernels  50.9 us (82%)
  local copies, waits for them, and re-layouts  10.7 us (17%)
    pallas_call x1, Pallas kernels, per_device(): pl.pallas_call(functools.partial(kernel, n, heads, groups, slots, rank),...  50.9 us
    unnamed x21, local copies, waits for them, and re-layouts  10.7 us

profile of v1, /device:TPU:30, one launch (start us, length us, event | category | flops | bytes accessed | tf_op | source)
XLA Modules:
  0.0 61.7 jit_solution(16595161260480526679)
XLA Ops:
  0.0 0.0 copy-start
  0.0 1.6 %copy-done = bf16[128,8192]{1,0:T(8,128)(2,1)S(1)} copy-done((bf16[128,8192]{1,0:T(8,128)(2,1)S(1)}, bf16[128,8192]{1,0:T(8,128)(2,1)}, u32[]{:S(2)}) %copy-start) | copy-done | bytes 2097176
  1.6 0.0 copy-start.1
  1.6 1.4 %copy-done.1 = bf16[2,8192,48]{1,2,0:T(8,128)(2,1)S(1)} copy-done((bf16[2,8192,48]{1,2,0:T(8,128)(2,1)S(1)}, bf16[2,8192,48]{1,2,0:T(8,128)(2,1)}, u32[]{:S(2)}) %copy-start.1) | copy-done | bytes 1572888
  3.0 0.0 copy-start.2
  3.0 1.0 %copy-done.2 = bf16[128,2,8,128]{3,2,1,0:T(8,128)(2,1)S(1)} copy-done((bf16[128,2,8,128]{3,2,1,0:T(8,128)(2,1)S(1)}, bf16[128,2,8,128]{3,2,1,0:T(8,128)(2,1)}, u32[]{:S(2)}) %copy-start.2) | copy-done | bytes 524312
  4.0 0.0 copy-start.3
  4.0 0.9 %copy-done.3 = bf16[4,16,2,8,128]{4,3,2,1,0:T(8,128)(2,1)S(1)} copy-done((bf16[4,16,2,8,128]{4,3,2,1,0:T(8,128)(2,1)S(1)}, bf16[4,16,2,8,128]{4,3,2,1,0:T(8,128)(2,1)}, u32[]{:S(2)}) %copy-start.3) | copy-done | bytes 262168
  5.0 0.0 copy-start.4
  5.0 0.9 %copy-done.4 = bf16[512,2,128]{2,1,0:T(2,128)(2,1)S(1)} copy-done((bf16[512,2,128]{2,1,0:T(2,128)(2,1)S(1)}, bf16[512,2,128]{2,1,0:T(2,128)(2,1)}, u32[]{:S(2)}) %copy-start.4) | copy-done | bytes 262168
  5.9 0.0 copy-start.5
  5.9 0.9 %copy-done.5 = bf16[512,2,128]{2,1,0:T(2,128)(2,1)S(1)} copy-done((bf16[512,2,128]{2,1,0:T(2,128)(2,1)S(1)}, bf16[512,2,128]{2,1,0:T(2,128)(2,1)}, u32[]{:S(2)}) %copy-start.5) | copy-done | bytes 262168
  6.9 0.0 copy-start.6
  6.9 0.9 %copy-done.6 = bf16[128,2,2,128]{3,2,1,0:T(2,128)(2,1)S(1)} copy-done((bf16[128,2,2,128]{3,2,1,0:T(2,128)(2,1)S(1)}, bf16[128,2,2,128]{3,2,1,0:T(2,128)(2,1)}, u32[]{:S(2)}) %copy-start.6) | copy-done | bytes 131096
  7.8 0.0 copy-start.7
  7.8 0.8 %copy-done.7 = bf16[4,16,2,2,128]{4,3,2,1,0:T(2,128)(2,1)S(1)} copy-done((bf16[4,16,2,2,128]{4,3,2,1,0:T(2,128)(2,1)S(1)}, bf16[4,16,2,2,128]{4,3,2,1,0:T(2,128)(2,1)}, u32[]{:S(2)}) %copy-start.7) | copy-done | bytes 65560
  8.6 0.0 copy-start.8
  8.6 0.7 %copy-done.8 = s32[1,128]{1,0:T(1,128)S(1)} copy-done((s32[1,128]{1,0:T(1,128)S(1)}, s32[1,128]{1,0:T(1,128)}, u32[]{:S(2)}) %copy-start.8) | copy-done | bytes 536
  9.3 0.0 copy-start.9
  9.3 0.7 %copy-done.9 = s32[4]{0:T(128)S(1)} copy-done((s32[4]{0:T(128)S(1)}, s32[4]{0:T(128)}, u32[]{:S(2)}) %copy-start.9) | copy-done | bytes 40
  10.0 50.9 %shard_map.100 = bf16[2048,128]{1,0:T(8,128)(2,1)S(1)} custom-call(bf16[128,8192]{1,0:T(8,128)(2,1)S(1)} %copy-done, bf16[96,8192]{1,0:T(8,128)(2,1)S(1)} %bitcast.11, bf16[1024,128]{1,0:T(8,128)(2,1)S(1)} %bitcast.13, bf16[256,128]{1,0:T(8,128)(2,1)S(1)} %bitcast.17, bf16[2048,128]{1,0:T(8,128)(2,1)S(1)} %bitcast.12, bf16[512,128]{1,0:T(8,128)(2,1)S(1)} %bitcast.16, ...), custom_call_target="tpu_custom_call" | custom-call | tf_op jit(solution)/shard_map/pallas_call | solution.py:265
  60.9 0.8 %copy.12 = bf16[128,2,8,128]{3,2,1,0:T(8,128)(2,1)} copy(bf16[128,2,8,128]{3,2,1,0:T(8,128)(2,1)S(1)} %bitcast.10) | data formatting | bytes 1048576
Async XLA Ops:
  0.0 1.6 %copy-start = (bf16[128,8192]{1,0:T(8,128)(2,1)S(1)}, bf16[128,8192]{1,0:T(8,128)(2,1)}, u32[]{:S(2)}) copy-start(bf16[128,8192]{1,0:T(8,128)(2,1)} %tok_hbm.1) | copy-start | bytes 6291460
  1.6 1.4 %copy-start.1 = (bf16[2,8192,48]{1,2,0:T(8,128)(2,1)S(1)}, bf16[2,8192,48]{1,2,0:T(8,128)(2,1)}, u32[]{:S(2)}) copy-start(bf16[2,8192,48]{1,2,0:T(8,128)(2,1)} %param.11) | copy-start | bytes 4718596
  3.0 1.0 %copy-start.2 = (bf16[128,2,8,128]{3,2,1,0:T(8,128)(2,1)S(1)}, bf16[128,2,8,128]{3,2,1,0:T(8,128)(2,1)}, u32[]{:S(2)}) copy-start(bf16[128,2,8,128]{3,2,1,0:T(8,128)(2,1)} %param.14) | copy-start | bytes 1572868
  4.0 0.9 %copy-start.3 = (bf16[4,16,2,8,128]{4,3,2,1,0:T(8,128)(2,1)S(1)}, bf16[4,16,2,8,128]{4,3,2,1,0:T(8,128)(2,1)}, u32[]{:S(2)}) copy-start(bf16[4,16,2,8,128]{4,3,2,1,0:T(8,128)(2,1)} %param.12) | copy-start | bytes 786436
  5.0 0.9 %copy-start.4 = (bf16[512,2,128]{2,1,0:T(2,128)(2,1)S(1)}, bf16[512,2,128]{2,1,0:T(2,128)(2,1)}, u32[]{:S(2)}) copy-start(bf16[512,2,128]{2,1,0:T(2,128)(2,1)} %param.16) | copy-start | bytes 786436
  5.9 0.9 %copy-start.5 = (bf16[512,2,128]{2,1,0:T(2,128)(2,1)S(1)}, bf16[512,2,128]{2,1,0:T(2,128)(2,1)}, u32[]{:S(2)}) copy-start(bf16[512,2,128]{2,1,0:T(2,128)(2,1)} %param.17) | copy-start | bytes 786436
  6.9 0.9 %copy-start.6 = (bf16[128,2,2,128]{3,2,1,0:T(2,128)(2,1)S(1)}, bf16[128,2,2,128]{3,2,1,0:T(2,128)(2,1)}, u32[]{:S(2)}) copy-start(bf16[128,2,2,128]{3,2,1,0:T(2,128)(2,1)} %param.15) | copy-start | bytes 393220
  7.8 0.8 %copy-start.7 = (bf16[4,16,2,2,128]{4,3,2,1,0:T(2,128)(2,1)S(1)}, bf16[4,16,2,2,128]{4,3,2,1,0:T(2,128)(2,1)}, u32[]{:S(2)}) copy-start(bf16[4,16,2,2,128]{4,3,2,1,0:T(2,128)(2,1)} %param.13) | copy-start | bytes 196612
  8.6 0.7 %copy-start.8 = (s32[1,128]{1,0:T(1,128)S(1)}, s32[1,128]{1,0:T(1,128)}, u32[]{:S(2)}) copy-start(s32[1,128]{1,0:T(1,128)} %slot_ref.1) | copy-start | bytes 1540
  9.3 0.7 %copy-start.9 = (s32[4]{0:T(128)S(1)}, s32[4]{0:T(128)}, u32[]{:S(2)}) copy-start(s32[4]{0:T(128)} %len_ref.1) | copy-start | bytes 52

commit v2 on v1

--- a/solution.py
+++ b/solution.py
@@ -24,9 +24,10 @@
 
 def kernel(
     n, heads, groups, slots, rank,
-    tok_hbm, down_hbm, aq_ref, akv_ref, qb_ref, kvb_ref, ck_hbm, cv_hbm, slot_ref, len_ref,
+    tok_hbm, down_hbm, aq_hbm, akv_hbm, qb_hbm, kvb_hbm, ck_hbm, cv_hbm, slot_hbm, len_hbm,
     out_ref,
-    tok_v, down_v, raw, kv, q, acc, top, total, xch, local_sem,
+    tok_v, down_v, raw, aq_ref, akv_ref, qb_ref, kvb_ref, slot_ref, len_ref,
+    kv, q, acc, top, total, xch, local_sem,
     send_rc, recv_rc, send_rf, recv_rf, send_lc, recv_lc, send_x, recv_x,
 ):
     me = lax.axis_index("ctx")
@@ -43,7 +44,14 @@
     load_v = pltpu.make_async_copy(cv_hbm, raw.at[1], local_sem.at[1])
     load_t = pltpu.make_async_copy(tok_hbm, tok_v, local_sem.at[2])
     load_d = pltpu.make_async_copy(down_hbm, down_v, local_sem.at[3])
-    for load in (load_k, load_v, load_t, load_d):
+    loads = [load_k, load_v, load_t, load_d]
+    small = [
+        pltpu.make_async_copy(source, target, local_sem.at[4 + i])
+        for i, (source, target) in enumerate((
+            (slot_hbm, slot_ref), (len_hbm, len_ref), (akv_hbm, akv_ref), (kvb_hbm, kvb_ref),
+            (aq_hbm, aq_ref), (qb_hbm, qb_ref)))
+    ]
+    for load in loads + small:
         load.start()
 
     barrier = pltpu.get_barrier_semaphore()
@@ -100,6 +108,8 @@
 
     load_t.wait()
     load_d.wait()
+    for load in small:
+        load.wait()
     slot = slot_ref[...]
     own = dot(down_v[...], tok_v[...], 1, 1).astype(BF16).astype(F32)
     part = jnp.zeros((width, toks), F32)
@@ -259,29 +269,34 @@
     down = jnp.swapaxes(adapter_down, 1, 2).reshape(-1, depth)
     vmem = pl.BlockSpec(memory_space=pltpu.VMEM)
     hbm = pl.BlockSpec(memory_space=pl.ANY)
-    smem = pl.BlockSpec(memory_space=pltpu.SMEM)
     dma = pltpu.SemaphoreType.DMA
     q_rows = toks * groups
     out = pl.pallas_call(
         functools.partial(kernel, n, heads, groups, slots, rank),
         out_shape=jax.ShapeDtypeStruct((toks * heads * groups, hd), BF16),
-        in_specs=[hbm, hbm, vmem, vmem, vmem, vmem, hbm, hbm, vmem, smem],
+        in_specs=[hbm] * 10,
         out_specs=vmem,
         scratch_shapes=[
             pltpu.VMEM((toks, depth), BF16),
             pltpu.VMEM(down.shape, BF16),
             pltpu.VMEM((2, cached * heads, hd), BF16),
+            pltpu.VMEM((slots * rank * heads * groups, hd), BF16),
+            pltpu.VMEM((slots * rank * heads * 2, hd), BF16),
+            pltpu.VMEM((toks * heads * groups, hd), BF16),
+            pltpu.VMEM((toks * heads * 2, hd), BF16),
+            pltpu.VMEM(adapter_slot.shape, jnp.int32),
+            pltpu.SMEM(cached_length.shape, jnp.int32),
             pltpu.VMEM((n, heads, 2, cached + toks, hd), BF16),
             pltpu.VMEM((heads, q_rows, hd), BF16),
             pltpu.VMEM((heads, hd, q_rows), F32),
             pltpu.VMEM((heads, 1, q_rows), F32),
             pltpu.VMEM((heads, 1, q_rows), F32),
             pltpu.VMEM((2, 3 * rank, toks), F32),
-            dma((4,)),
+            dma((10,)),
             dma((n,)), dma((n,)), dma((n,)), dma((n,)), dma((n,)), dma((n,)), dma, dma,
         ],
         compiler_params=pltpu.CompilerParams(
-            collective_id=0, has_side_effects=True, vmem_limit_bytes=48 * 1024 * 1024),
+            collective_id=0, has_side_effects=True, vmem_limit_bytes=60 * 1024 * 1024),
     )(
         tokens, down,
         adapter_query.reshape(-1, hd), adapter_keyvalue.reshape(-1, hd),

time: 62.1 us -> 53.1 us (0.86)
  local copies, waits for them, and re-layouts: 10.7 us -> 1.87 us
    unnamed x21 -> x1, local copies, waits for them, and re-layouts: 10.7 us -> 1.87 us
where the time goes in v2:
time: 53.1 us; the launch traced here: 53 us
  Pallas kernels  51.1 us (96%)
  local copies, waits for them, and re-layouts  1.87 us (4%)
    pallas_call x1, Pallas kernels, per_device(): pl.pallas_call(functools.partial(kernel, n, heads, groups, slots, rank),...  51.1 us
    unnamed x1, local copies, waits for them, and re-layouts  1.87 us

profile of v2, /device:TPU:30, one launch (start us, length us, event | category | flops | bytes accessed | tf_op | source)
XLA Modules:
  0.0 53.0 jit_solution(4220221188345644551)
XLA Ops:
  0.0 51.1 %shard_map.100 = bf16[2048,128]{1,0:T(8,128)(2,1)} custom-call(bf16[128,8192]{1,0:T(8,128)(2,1)} %tok_hbm.1, bf16[96,8192]{1,0:T(8,128)(2,1)} %bitcast.11, bf16[1024,128]{1,0:T(8,128)(2,1)} %bitcast.13, bf16[256,128]{1,0:T(8,128)(2,1)} %bitcast.17, bf16[2048,128]{1,0:T(8,128)(2,1)} %bitcast.12, bf16[512,128]{1,0:T(8,128)(2,1)} %bitcast.16, ...), custom_call_target="tpu_custom_call" | custom-call | tf_op jit(solution)/shard_map/pallas_call | solution.py:274
  51.1 1.9 %copy.12 = bf16[128,2,8,128]{3,2,1,0:T(8,128)(2,1)} copy(bf16[128,2,8,128]{3,2,1,0:T(8,128)(2,1)} %bitcast.10) | data formatting | bytes 1048576

commit v3 on v2

--- a/solution.py
+++ b/solution.py
@@ -27,10 +27,17 @@
     tok_hbm, down_hbm, aq_hbm, akv_hbm, qb_hbm, kvb_hbm, ck_hbm, cv_hbm, slot_hbm, len_hbm,
     out_ref,
     tok_v, down_v, raw, aq_ref, akv_ref, qb_ref, kvb_ref, slot_ref, len_ref,
-    kv, q, acc, top, total, xch, local_sem,
+    kv, q, acc, top, total, xch, done, local_sem,
     send_rc, recv_rc, send_rf, recv_rf, send_lc, recv_lc, send_x, recv_x,
+    send_q, recv_q, send_f, recv_f, send_o, recv_o,
 ):
+    handed = heads > 1 and n > 3
     me = lax.axis_index("ctx")
+    last = n - 1
+    at_end = ((me == 0) | (me == last)) & handed
+    helper = ((me == 1) | (me == last - 1)) & handed
+    inner = jnp.where(me == 0, 1, last - 1)
+    outer = jnp.where(me == 1, 0, last)
     rep = lax.axis_index("rep")
     toks = tok_v.shape[0]
     cached = ck_hbm.shape[0] // heads
@@ -67,23 +74,59 @@
 
     neighbours = 1 + jnp.where(me > 0, 1, 0) + jnp.where(me < n - 1, 1, 0)
 
-    def cached_right(src):
-        part = kv.at[src, :, :, pl.ds(0, cached)]
+    def hop(part, send, recv, to):
         return pltpu.make_async_remote_copy(
-            src_ref=part, dst_ref=part, send_sem=send_rc.at[src], recv_sem=recv_rc.at[src],
-            device_id={"ctx": me + 1}, device_id_type=MESH)
-
-    def fresh_right(src):
-        part = kv.at[src, :, :, pl.ds(cached, toks)]
+            src_ref=part, dst_ref=part, send_sem=send, recv_sem=recv,
+            device_id={"ctx": to}, device_id_type=MESH)
+
+    def cached_right(src, h):
+        part = kv.at[src, h, :, pl.ds(0, cached)]
+        return hop(part, send_rc.at[src, h], recv_rc.at[src, h], me + 1)
+
+    def fresh_right(src, h):
+        part = kv.at[src, h, :, pl.ds(cached, toks)]
+        return hop(part, send_rf.at[src, h], recv_rf.at[src, h], me + 1)
+
+    def cached_left(src, h):
+        part = kv.at[src, h, :, pl.ds(0, cached)]
+        return hop(part, send_lc.at[src, h], recv_lc.at[src, h], me - 1)
+
+    def query_in():
         return pltpu.make_async_remote_copy(
-            src_ref=part, dst_ref=part, send_sem=send_rf.at[src], recv_sem=recv_rf.at[src],
-            device_id={"ctx": me + 1}, device_id_type=MESH)
-
-    def cached_left(src):
-        part = kv.at[src, :, :, pl.ds(0, cached)]
+            src_ref=q.at[0], dst_ref=q.at[heads], send_sem=send_q, recv_sem=recv_q,
+            device_id={"ctx": inner}, device_id_type=MESH)
+
+    def fresh_in():
+        return hop(kv.at[last, 0, :, pl.ds(cached, toks)], send_f, recv_f, inner)
+
+    def result_out():
         return pltpu.make_async_remote_copy(
-            src_ref=part, dst_ref=part, send_sem=send_lc.at[src], recv_sem=recv_lc.at[src],
-            device_id={"ctx": me - 1}, device_id_type=MESH)
+            src_ref=done.at[0], dst_ref=done.at[1], send_sem=send_o, recv_sem=recv_o,
+            device_id={"ctx": outer}, device_id_type=MESH)
+
+    def given(h):
+        return handed and h == 0
+
+    def to_right(h):
+        return me < (last - 1 if given(h) else last)
+
+    def to_left(h):
+        return me > (1 if given(h) else 0)
+
+    def from_left(h):
+        return (me > 0) & (me < last) if given(h) else me > 0
+
+    def from_right(h):
+        return (me > 0) & (me < last) if given(h) else me < last
+
+    def send_cached(h):
+        @pl.when(to_right(h))
+        def _():
+            cached_right(me, h).start()
+
+        @pl.when(to_left(h))
+        def _():
+            cached_left(me, h).start()
 
     step = 128
     load_k.wait()
@@ -95,16 +138,13 @@
             for b in range(cached // step):
                 block = raw[c, pl.ds(b * step * heads, step * heads), :]
                 kv[me, h, c, pl.ds(b * step, step), :] = dot(pick, block).astype(BF16)
-
-    pl.semaphore_wait(barrier, neighbours)
-
-    @pl.when(me < n - 1)
-    def _():
-        cached_right(me).start()
-
-    @pl.when(me > 0)
-    def _():
-        cached_left(me).start()
+        if h == 0:
+            pl.semaphore_wait(barrier, neighbours)
+            send_cached(0)
+        else:
+            @pl.when(jnp.logical_not(at_end))
+            def _():
+                send_cached(h)
 
     load_t.wait()
     load_d.wait()
@@ -146,9 +186,15 @@
             base = dot(pick.astype(F32).astype(BF16), kvb)
             kv[me, h, c, pl.ds(cached, toks), :] = (base + delta).astype(BF16)
 
-    @pl.when(me < n - 1)
-    def _():
-        fresh_right(me).start()
+    for h in range(heads):
+        if given(h):
+            @pl.when(me == last)
+            def _():
+                fresh_in().start()
+
+        @pl.when(to_right(h) & (jnp.logical_not(at_end) | (h == 0)))
+        def _():
+            fresh_right(me, h).start()
 
     each = heads * groups
     wide = dot(spread(shrunk[0:rank]), expand(each), 0, 0)
@@ -161,6 +207,16 @@
         delta = dot(jnp.where(keep, wide, 0.0).astype(BF16), aq)
         base = base_all[:, h * groups:(h + 1) * groups].reshape(q_rows, hd)
         q[h] = (base + delta).astype(BF16)
+        if given(h):
+            @pl.when(at_end)
+            def _():
+                query_in().start()
+                for other in range(1, heads):
+                    send_cached(other)
+
+                    @pl.when(to_right(other))
+                    def _():
+                        fresh_right(me, other).start()
 
     top[...] = jnp.full(top.shape, FILL, F32)
     total[...] = jnp.zeros(total.shape, F32)
@@ -168,90 +224,145 @@
     tiles = q_rows // TILE
     scale = hd ** -0.5
 
-    def process(src, rows, causal):
+    def process(src, rows, head_of, slot_of, low, high):
         limit = len_ref[src]
 
         def body(index, carry):
-            h = index // tiles
+            k = index // tiles
             j = index % tiles
+            h = head_of(k)
+            slot = slot_of(k)
+            asker = jnp.where(slot == heads, outer, me)
             cols = pl.ds(pl.multiple_of(j * TILE, TILE), TILE)
-            scores = dot(kv[src, h, 0, pl.ds(0, rows), :], q[h, cols, :], 1, 1) * scale
+            scores = dot(kv[src, h, 0, pl.ds(0, rows), :], q[slot, cols, :], 1, 1) * scale
             row = iota(scores.shape, 0)
             seen = row < limit
             if rows > cached:
-                if causal:
-                    token = lax.div(j * TILE + iota(scores.shape, 1), groups)
-                    seen = seen & (row < cached) | (row >= cached) & (row - cached <= token)
-                else:
-                    seen = seen | (row >= cached)
+                reach = (asker - src) * toks + lax.div(j * TILE + iota(scores.shape, 1), groups)
+                seen = seen & (row < cached) | (row >= cached) & (row - cached <= reach)
             scores = jnp.where(seen, scores, FILL)
-            old = top[h, :, cols]
+            old = top[slot, :, cols]
             new = jnp.maximum(old, jnp.max(scores, axis=0, keepdims=True))
             weights = jnp.exp(scores - new)
             factor = jnp.exp(old - new)
-            top[h, :, cols] = new
-            total[h, :, cols] = total[h, :, cols] * factor + jnp.sum(weights, axis=0, keepdims=True)
-            acc[h, :, cols] = acc[h, :, cols] * factor + dot(
+            top[slot, :, cols] = new
+            total[slot, :, cols] = total[slot, :, cols] * factor + jnp.sum(
+                weights, axis=0, keepdims=True)
+            acc[slot, :, cols] = acc[slot, :, cols] * factor + dot(
                 kv[src, h, 1, pl.ds(0, rows), :], weights.astype(BF16), 0, 0)
             return carry
 
-        lax.fori_loop(0, heads * tiles, body, 0)
-
-    process(me, rows_all, True)
+        lax.fori_loop(low * tiles, high * tiles, body, 0)
+
+    own = jnp.where(at_end, 1, 0)
+    process(me, rows_all, lambda k: k, lambda k: k, own, heads)
+    asked = 1 + jnp.where(helper, 1, 0)
+
+    def finished(slot):
+        return (acc[slot] / total[slot]).T
 
     def arrive(t, carry):
-        @pl.when(me - t >= 0)
-        def _():
-            cached_right(me - t).wait_recv()
-
-            @pl.when(me < n - 1)
-            def _():
-                cached_right(me - t).start()
-
-            fresh_right(me - t).wait_recv()
-
-            @pl.when(me < n - 1)
-            def _():
-                fresh_right(me - t).start()
-
-        @pl.when(me + t < n)
-        def _():
-            cached_left(me + t).wait_recv()
-
-            @pl.when(me > 0)
-            def _():
-                cached_left(me + t).start()
-
-        @pl.when(me - t >= 0)
-        def _():
-            process(me - t, rows_all, False)
-
-        @pl.when(me + t < n)
-        def _():
-            process(me + t, cached, False)
+        left = me - t
+        right = me + t
+        for h in range(heads):
+            @pl.when(from_left(h) & (left >= 0))
+            def _():
+                cached_right(left, h).wait_recv()
+
+                @pl.when(to_right(h))
+                def _():
+                    cached_right(left, h).start()
+
+                fresh_right(left, h).wait_recv()
+
+                @pl.when(to_right(h))
+                def _():
+                    fresh_right(left, h).start()
+
+            @pl.when(from_right(h) & (right < n))
+            def _():
+                cached_left(right, h).wait_recv()
+
+                @pl.when(to_left(h))
+                def _():
+                    cached_left(right, h).start()
+
+            if given(h):
+                @pl.when(helper & (t == 1))
+                def _():
+                    query_in().wait_recv()
+
+                    @pl.when(me == last - 1)
+                    def _():
+                        fresh_in().wait_recv()
+
+                    process(me, rows_all, lambda k: 0, lambda k: heads, 0, 1)
+
+                    @pl.when(me == last - 1)
+                    def _():
+                        process(last, rows_all, lambda k: 0, lambda k: heads, 0, 1)
+
+            slot_of = (lambda k: jnp.where(k == 0, 0, heads)) if given(h) else (lambda k: h)
+            count = asked if given(h) else 1
+
+            @pl.when(from_left(h) & (left >= 0))
+            def _():
+                process(left, rows_all, lambda k: h, slot_of, 0, count)
+
+            @pl.when(from_right(h) & (right < n))
+            def _():
+                many = jnp.where(right == last, 1, count) if given(h) else count
+                many = jnp.where(me == last - 1, many, count)
+                process(right, cached, lambda k: h, slot_of, 0, many)
+
+            if given(h):
+                @pl.when(helper & (t == n - 2))
+                def _():
+                    done[0] = finished(heads).astype(BF16)
+                    result_out().start()
 
         return carry
 
     lax.fori_loop(1, n, arrive, 0)
 
-    results = []
-    for h in range(heads):
-        result = (acc[h] / total[h]).T
-        results.append(result.reshape(toks, groups, hd))
+    @pl.when(at_end)
+    def _():
+        result_out().wait_recv()
+
+    @pl.when(jnp.logical_not(at_end))
+    def _():
+        done[1] = finished(0).astype(BF16)
+
+    results = [done[1].astype(F32).reshape(toks, groups, hd)]
+    for h in range(1, heads):
+        results.append(finished(h).reshape(toks, groups, hd))
     result = jnp.concatenate(results, axis=1) if heads > 1 else results[0]
     out_ref[...] = result.reshape(toks * heads * groups, hd).astype(BF16)
 
     swap.wait_send()
+    if handed:
+        @pl.when(at_end)
+        def _():
+            query_in().wait_send()
+
+        @pl.when(me == last)
+        def _():
+            fresh_in().wait_send()
+
+        @pl.when(helper)
+        def _():
+            result_out().wait_send()
 
     def drain(t, carry):
-        @pl.when((me - t >= 0) & (me < n - 1))
-        def _():
-            cached_right(me - t).wait_send()
-            fresh_right(me - t).wait_send()
-
-        @pl.when((me + t < n) & (me > 0))
-        def _():
-            cached_left(me + t).wait_send()
+        for h in range(heads):
+            @pl.when((me - t >= 0) & to_right(h))
+            def _():
+                cached_right(me - t, h).wait_send()
+                fresh_right(me - t, h).wait_send()
+
+            @pl.when((me + t < n) & to_left(h))
+            def _():
+                cached_left(me + t, h).wait_send()
 
         return carry
 
@@ -287,13 +398,14 @@
             pltpu.VMEM(adapter_slot.shape, jnp.int32),
             pltpu.SMEM(cached_length.shape, jnp.int32),
             pltpu.VMEM((n, heads, 2, cached + toks, hd), BF16),
-            pltpu.VMEM((heads, q_rows, hd), BF16),
-            pltpu.VMEM((heads, hd, q_rows), F32),
-            pltpu.VMEM((heads, 1, q_rows), F32),
-            pltpu.VMEM((heads, 1, q_rows), F32),
+            pltpu.VMEM((heads + 1, q_rows, hd), BF16),
+            pltpu.VMEM((heads + 1, hd, q_rows), F32),
+            pltpu.VMEM((heads + 1, 1, q_rows), F32),
+            pltpu.VMEM((heads + 1, 1, q_rows), F32),
             pltpu.VMEM((2, 3 * rank, toks), F32),
+            pltpu.VMEM((2, q_rows, hd), BF16),
             dma((10,)),
-            dma((n,)), dma((n,)), dma((n,)), dma((n,)), dma((n,)), dma((n,)), dma, dma,
+            *[dma((n, heads))] * 6, *[dma] * 8,
         ],
         compiler_params=pltpu.CompilerParams(
             collective_id=0, has_side_effects=True, vmem_limit_bytes=60 * 1024 * 1024),

time: 53.1 us -> 57.4 us (1.081)
  Pallas kernels: 51.1 us -> 55.4 us
    pallas_call x1, Pallas kernels: 51.1 us -> 55.4 us  [per_device(): pl.pallas_call(functools.partial(kernel, n, heads, groups, slots, rank),...]
where the time goes in v3:
time: 57.4 us; the launch traced here: 57.3 us
  Pallas kernels  55.4 us (97%)
  local copies, waits for them, and re-layouts  1.87 us (3%)
    pallas_call x1, Pallas kernels, per_device(): pl.pallas_call(functools.partial(kernel, n, heads, groups, slots, rank),...  55.4 us
    unnamed x1, local copies, waits for them, and re-layouts  1.87 us

profile of v3, /device:TPU:30, one launch (start us, length us, event | category | flops | bytes accessed | tf_op | source)
XLA Modules:
  0.0 57.3 jit_solution(16781955619703602027)
XLA Ops:
  0.0 55.4 %shard_map.100 = bf16[2048,128]{1,0:T(8,128)(2,1)} custom-call(bf16[128,8192]{1,0:T(8,128)(2,1)} %tok_hbm.1, bf16[96,8192]{1,0:T(8,128)(2,1)} %bitcast.11, bf16[1024,128]{1,0:T(8,128)(2,1)} %bitcast.13, bf16[256,128]{1,0:T(8,128)(2,1)} %bitcast.17, bf16[2048,128]{1,0:T(8,128)(2,1)} %bitcast.12, bf16[512,128]{1,0:T(8,128)(2,1)} %bitcast.16, ...), custom_call_target="tpu_custom_call" | custom-call | tf_op jit(solution)/shard_map/pallas_call | solution.py:385
  55.4 1.9 %copy.12 = bf16[128,2,8,128]{3,2,1,0:T(8,128)(2,1)} copy(bf16[128,2,8,128]{3,2,1,0:T(8,128)(2,1)} %bitcast.10) | data formatting | bytes 1048576

commit v4 on v3

--- a/solution.py
+++ b/solution.py
@@ -10,6 +10,8 @@
 FILL = -1e30
 MESH = pl.DeviceIdType.MESH
 TILE = 256
+ABREAST = 4
+LOG2_E = 1.4426950408889634
 F32 = jnp.float32
 BF16 = jnp.bfloat16
 
@@ -221,38 +223,42 @@
     top[...] = jnp.full(top.shape, FILL, F32)
     total[...] = jnp.zeros(total.shape, F32)
     acc[...] = jnp.zeros(acc.shape, F32)
-    tiles = q_rows // TILE
-    scale = hd ** -0.5
+    turns = q_rows // (TILE * ABREAST)
+    scale = hd ** -0.5 * LOG2_E
 
     def process(src, rows, head_of, slot_of, low, high):
         limit = len_ref[src]
 
         def body(index, carry):
-            k = index // tiles
-            j = index % tiles
+            k = index // turns
             h = head_of(k)
             slot = slot_of(k)
             asker = jnp.where(slot == heads, outer, me)
-            cols = pl.ds(pl.multiple_of(j * TILE, TILE), TILE)
-            scores = dot(kv[src, h, 0, pl.ds(0, rows), :], q[slot, cols, :], 1, 1) * scale
-            row = iota(scores.shape, 0)
-            seen = row < limit
-            if rows > cached:
-                reach = (asker - src) * toks + lax.div(j * TILE + iota(scores.shape, 1), groups)
-                seen = seen & (row < cached) | (row >= cached) & (row - cached <= reach)
-            scores = jnp.where(seen, scores, FILL)
-            old = top[slot, :, cols]
-            new = jnp.maximum(old, jnp.max(scores, axis=0, keepdims=True))
-            weights = jnp.exp(scores - new)
-            factor = jnp.exp(old - new)
-            top[slot, :, cols] = new
-            total[slot, :, cols] = total[slot, :, cols] * factor + jnp.sum(
-                weights, axis=0, keepdims=True)
-            acc[slot, :, cols] = acc[slot, :, cols] * factor + dot(
-                kv[src, h, 1, pl.ds(0, rows), :], weights.astype(BF16), 0, 0)
+            starts = [(index % turns * ABREAST + i) * TILE for i in range(ABREAST)]
+            spans = [pl.ds(pl.multiple_of(start, TILE), TILE) for start in starts]
+            keys = kv[src, h, 0, pl.ds(0, rows), :]
+            values = kv[src, h, 1, pl.ds(0, rows), :]
+            row = iota((rows, TILE), 0)
+            wide = [dot(keys, q[slot, cols, :], 1, 1) for cols in spans]
+            for start, cols, scores in zip(starts, spans, wide):
+                seen = row < limit
+                if rows > cached:
+                    reach = (asker - src) * toks + lax.div(
+                        start + iota((1, TILE), 1), groups) + cached
+                    seen = seen & (row < cached) | (row >= cached) & (row <= reach)
+                scores = jnp.where(seen, scores, FILL)
+                old = top[slot, :, cols]
+                new = jnp.maximum(old, jnp.max(scores, axis=0, keepdims=True))
+                weights = jnp.exp2(scores * scale - new * scale)
+                factor = jnp.exp2((old - new) * scale)
+                top[slot, :, cols] = new
+                total[slot, :, cols] = total[slot, :, cols] * factor + jnp.sum(
+                    weights, axis=0, keepdims=True)
+                acc[slot, :, cols] = acc[slot, :, cols] * factor + dot(
+                    values, weights.astype(BF16), 0, 0)
             return carry
 
-        lax.fori_loop(low * tiles, high * tiles, body, 0)
+        lax.fori_loop(low * turns, high * turns, body, 0)
 
     own = jnp.where(at_end, 1, 0)
     process(me, rows_all, lambda k: k, lambda k: k, own, heads)

time: 57.4 us -> 47.9 us (0.83)
  Pallas kernels: 55.4 us -> 45.9 us
    pallas_call x1, Pallas kernels: 55.4 us -> 45.9 us  [per_device(): pl.pallas_call(functools.partial(kernel, n, heads, groups, slots, rank),...]
where the time goes in v4:
time: 47.9 us; the launch traced here: 47.8 us
  Pallas kernels  45.9 us (96%)
  local copies, waits for them, and re-layouts  1.87 us (4%)
    pallas_call x1, Pallas kernels, per_device(): pl.pallas_call(functools.partial(kernel, n, heads, groups, slots, rank),...  45.9 us
    unnamed x1, local copies, waits for them, and re-layouts  1.87 us

profile of v4, /device:TPU:30, one launch (start us, length us, event | category | flops | bytes accessed | tf_op | source)
XLA Modules:
  0.0 47.8 jit_solution(8881607606199645067)
XLA Ops:
  0.0 45.9 %shard_map.100 = bf16[2048,128]{1,0:T(8,128)(2,1)} custom-call(bf16[128,8192]{1,0:T(8,128)(2,1)} %tok_hbm.1, bf16[96,8192]{1,0:T(8,128)(2,1)} %bitcast.11, bf16[1024,128]{1,0:T(8,128)(2,1)} %bitcast.13, bf16[256,128]{1,0:T(8,128)(2,1)} %bitcast.17, bf16[2048,128]{1,0:T(8,128)(2,1)} %bitcast.12, bf16[512,128]{1,0:T(8,128)(2,1)} %bitcast.16, ...), custom_call_target="tpu_custom_call" | custom-call | tf_op jit(solution)/shard_map/pallas_call | solution.py:391
  45.9 1.9 %copy.12 = bf16[128,2,8,128]{3,2,1,0:T(8,128)(2,1)} copy(bf16[128,2,8,128]{3,2,1,0:T(8,128)(2,1)} %bitcast.10) | data formatting | bytes 1048576

commit v5 on v4

--- a/solution.py
+++ b/solution.py
@@ -121,12 +121,12 @@
     def from_right(h):
         return (me > 0) & (me < last) if given(h) else me < last
 
-    def send_cached(h):
-        @pl.when(to_right(h))
+    def send_cached(right, left, h):
+        @pl.when(right)
         def _():
             cached_right(me, h).start()
 
-        @pl.when(to_left(h))
+        @pl.when(left)
         def _():
             cached_left(me, h).start()
 
@@ -142,11 +142,11 @@
                 kv[me, h, c, pl.ds(b * step, step), :] = dot(pick, block).astype(BF16)
         if h == 0:
             pl.semaphore_wait(barrier, neighbours)
-            send_cached(0)
+            send_cached(to_right(0), to_left(0), 0)
         else:
-            @pl.when(jnp.logical_not(at_end))
-            def _():
-                send_cached(h)
+            early = jnp.logical_not(at_end)
+            ahead = jnp.logical_not(to_right(0)) if handed else True
+            send_cached(to_right(h) & early & ahead, to_left(h) & early, h)
 
     load_t.wait()
     load_d.wait()
@@ -198,6 +198,10 @@
         def _():
             fresh_right(me, h).start()
 
+    if handed:
+        for h in range(1, heads):
+            send_cached(to_right(h) & to_right(0) & jnp.logical_not(at_end), False, h)
+
     each = heads * groups
     wide = dot(spread(shrunk[0:rank]), expand(each), 0, 0)
     wide = jnp.broadcast_to(wide[:, None, :], (toks, groups, wide.shape[1]))
@@ -214,7 +218,7 @@
             def _():
                 query_in().start()
                 for other in range(1, heads):
-                    send_cached(other)
+                    send_cached(to_right(other), to_left(other), other)
 
                     @pl.when(to_right(other))
                     def _():
@@ -226,8 +230,9 @@
     turns = q_rows // (TILE * ABREAST)
     scale = hd ** -0.5 * LOG2_E
 
-    def process(src, rows, head_of, slot_of, low, high):
+    def process(src, span, head_of, slot_of, low, high):
         limit = len_ref[src]
+        first, rows = span
 
         def body(index, carry):
             k = index // turns
@@ -236,13 +241,13 @@
             asker = jnp.where(slot == heads, outer, me)
             starts = [(index % turns * ABREAST + i) * TILE for i in range(ABREAST)]
             spans = [pl.ds(pl.multiple_of(start, TILE), TILE) for start in starts]
-            keys = kv[src, h, 0, pl.ds(0, rows), :]
-            values = kv[src, h, 1, pl.ds(0, rows), :]
-            row = iota((rows, TILE), 0)
+            keys = kv[src, h, 0, pl.ds(first, rows), :]
+            values = kv[src, h, 1, pl.ds(first, rows), :]
+            row = first + iota((rows, TILE), 0)
             wide = [dot(keys, q[slot, cols, :], 1, 1) for cols in spans]
             for start, cols, scores in zip(starts, spans, wide):
                 seen = row < limit
-                if rows > cached:
+                if first + rows > cached:
                     reach = (asker - src) * toks + lax.div(
                         start + iota((1, TILE), 1), groups) + cached
                     seen = seen & (row < cached) | (row >= cached) & (row <= reach)
@@ -260,9 +265,15 @@
 
         lax.fori_loop(low * turns, high * turns, body, 0)
 
+    both, old_part, new_part = (0, rows_all), (0, cached), (cached, toks)
     own = jnp.where(at_end, 1, 0)
-    process(me, rows_all, lambda k: k, lambda k: k, own, heads)
-    asked = 1 + jnp.where(helper, 1, 0)
+    process(me, both, lambda k: k, lambda k: k, own, heads)
+
+    def mine(src, span, h):
+        process(src, span, lambda k: h, lambda k: h, 0, 1)
+
+    def asked(src, span):
+        process(src, span, lambda k: 0, lambda k: heads, 0, 1)
 
     def finished(slot):
         return (acc[slot] / total[slot]).T
@@ -270,8 +281,12 @@
     def arrive(t, carry):
         left = me - t
         right = me + t
+        across = jnp.where(me == 1, right, left)
         for h in range(heads):
-            @pl.when(from_left(h) & (left >= 0))
+            on_left = from_left(h) & (left >= 0)
+            on_right = from_right(h) & (right < n)
+
+            @pl.when(on_left)
             def _():
                 cached_right(left, h).wait_recv()
 
@@ -279,53 +294,61 @@
                 def _():
                     cached_right(left, h).start()
 
+            @pl.when(on_right)
+            def _():
+                cached_left(right, h).wait_recv()
+
+                @pl.when(to_left(h))
+                def _():
+                    cached_left(right, h).start()
+
+            if given(h):
+                @pl.when(helper & (t > 1) & (t < n - 1))
+                def _():
+                    asked(across, old_part)
+            else:
+                @pl.when(on_left)
+                def _():
+                    mine(left, old_part, h)
+
+            @pl.when(on_left)
+            def _():
                 fresh_right(left, h).wait_recv()
 
                 @pl.when(to_right(h))
                 def _():
                     fresh_right(left, h).start()
 
-            @pl.when(from_right(h) & (right < n))
-            def _():
-                cached_left(right, h).wait_recv()
-
-                @pl.when(to_left(h))
-                def _():
-                    cached_left(right, h).start()
-
             if given(h):
-                @pl.when(helper & (t == 1))
-                def _():
-                    query_in().wait_recv()
-
-                    @pl.when(me == last - 1)
-                    def _():
-                        fresh_in().wait_recv()
-
-                    process(me, rows_all, lambda k: 0, lambda k: heads, 0, 1)
-
-                    @pl.when(me == last - 1)
-                    def _():
-                        process(last, rows_all, lambda k: 0, lambda k: heads, 0, 1)
-
-            slot_of = (lambda k: jnp.where(k == 0, 0, heads)) if given(h) else (lambda k: h)
-            count = asked if given(h) else 1
-
-            @pl.when(from_left(h) & (left >= 0))
-            def _():
-                process(left, rows_all, lambda k: h, slot_of, 0, count)
-
-            @pl.when(from_right(h) & (right < n))
-            def _():
-                many = jnp.where(right == last, 1, count) if given(h) else count
-                many = jnp.where(me == last - 1, many, count)
-                process(right, cached, lambda k: h, slot_of, 0, many)
-
-            if given(h):
+                @pl.when((me == last - 1) & (t > 1) & (t < n - 1))
+                def _():
+                    asked(across, new_part)
+
                 @pl.when(helper & (t == n - 2))
                 def _():
                     done[0] = finished(heads).astype(BF16)
                     result_out().start()
+
+            @pl.when(on_left)
+            def _():
+                mine(left, both if given(h) else new_part, h)
+
+            @pl.when(on_right)
+            def _():
+                mine(right, old_part, h)
+
+        if handed:
+            @pl.when(helper & (t == 1))
+            def _():
+                query_in().wait_recv()
+
+                @pl.when(me == last - 1)
+                def _():
+                    fresh_in().wait_recv()
+
+                asked(me, both)
+                asked(outer, both)
+                asked(across, both)
 
         return carry
 

time: 47.9 us -> 47.7 us (level)
  no operation moved by 1% of the time
where the time goes in v5:
time: 47.7 us; the launch traced here: 47.5 us
  Pallas kernels  45.6 us (96%)
  local copies, waits for them, and re-layouts  1.87 us (4%)
    pallas_call x1, Pallas kernels, per_device(): pl.pallas_call(functools.partial(kernel, n, heads, groups, slots, rank),...  45.6 us
    unnamed x1, local copies, waits for them, and re-layouts  1.87 us

profile of v5, /device:TPU:30, one launch (start us, length us, event | category | flops | bytes accessed | tf_op | source)
XLA Modules:
  0.0 47.5 jit_solution(3745374568222842442)
XLA Ops:
  0.0 45.6 %shard_map.100 = bf16[2048,128]{1,0:T(8,128)(2,1)} custom-call(bf16[128,8192]{1,0:T(8,128)(2,1)} %tok_hbm.1, bf16[96,8192]{1,0:T(8,128)(2,1)} %bitcast.11, bf16[1024,128]{1,0:T(8,128)(2,1)} %bitcast.13, bf16[256,128]{1,0:T(8,128)(2,1)} %bitcast.17, bf16[2048,128]{1,0:T(8,128)(2,1)} %bitcast.12, bf16[512,128]{1,0:T(8,128)(2,1)} %bitcast.16, ...), custom_call_target="tpu_custom_call" | custom-call | tf_op jit(solution)/shard_map/pallas_call | solution.py:414
  45.6 1.9 %copy.12 = bf16[128,2,8,128]{3,2,1,0:T(8,128)(2,1)} copy(bf16[128,2,8,128]{3,2,1,0:T(8,128)(2,1)} %bitcast.10) | data formatting | bytes 1048576

commit v6 on v5

--- a/solution.py
+++ b/solution.py
@@ -348,7 +348,14 @@
 
                 asked(me, both)
                 asked(outer, both)
-                asked(across, both)
+
+                @pl.when(me == 1)
+                def _():
+                    asked(across, old_part)
+
+                @pl.when(me == last - 1)
+                def _():
+                    asked(across, both)
 
         return carry
 
@@ -408,7 +415,7 @@
     cached = cached_keys.shape[0]
     down = jnp.swapaxes(adapter_down, 1, 2).reshape(-1, depth)
     vmem = pl.BlockSpec(memory_space=pltpu.VMEM)
-    hbm = pl.BlockSpec(memory_space=pl.ANY)
+    hbm = pl.BlockSpec(memory_space=pltpu.HBM)
     dma = pltpu.SemaphoreType.DMA
     q_rows = toks * groups
     out = pl.pallas_call(
@@ -437,7 +444,7 @@
             *[dma((n, heads))] * 6, *[dma] * 8,
         ],
         compiler_params=pltpu.CompilerParams(
-            collective_id=0, has_side_effects=True, vmem_limit_bytes=60 * 1024 * 1024),
+            collective_id=0, has_side_effects=True, vmem_limit_bytes=40 * 1024 * 1024),
     )(
         tokens, down,
         adapter_query.reshape(-1, hd), adapter_keyvalue.reshape(-1, hd),

time: 47.7 us -> 56.3 us (1.18)
  local copies, waits for them, and re-layouts: 1.87 us -> 10.7 us
    unnamed x1 -> x21, local copies, waits for them, and re-layouts: 1.87 us -> 10.7 us
where the time goes in v6:
time: 56.3 us; the launch traced here: 55.9 us
  Pallas kernels  45.1 us (80%)
  local copies, waits for them, and re-layouts  10.7 us (19%)
    pallas_call x1, Pallas kernels, per_device(): pl.pallas_call(functools.partial(kernel, n, heads, groups, slots, rank),...  45.1 us
    unnamed x21, local copies, waits for them, and re-layouts  10.7 us

profile of v6, /device:TPU:30, one launch (start us, length us, event | category | flops | bytes accessed | tf_op | source)
XLA Modules:
  0.0 55.9 jit_solution(2048519264985242323)
XLA Ops:
  0.0 0.0 copy-start
  0.0 1.6 %copy-done = bf16[128,8192]{1,0:T(8,128)(2,1)S(1)} copy-done((bf16[128,8192]{1,0:T(8,128)(2,1)S(1)}, bf16[128,8192]{1,0:T(8,128)(2,1)}, u32[]{:S(2)}) %copy-start) | copy-done | bytes 2097176
  1.6 0.0 copy-start.1
  1.6 1.4 %copy-done.1 = bf16[2,8192,48]{1,2,0:T(8,128)(2,1)S(1)} copy-done((bf16[2,8192,48]{1,2,0:T(8,128)(2,1)S(1)}, bf16[2,8192,48]{1,2,0:T(8,128)(2,1)}, u32[]{:S(2)}) %copy-start.1) | copy-done | bytes 1572888
  3.0 0.0 copy-start.2
  3.0 1.0 %copy-done.2 = bf16[128,2,8,128]{3,2,1,0:T(8,128)(2,1)S(1)} copy-done((bf16[128,2,8,128]{3,2,1,0:T(8,128)(2,1)S(1)}, bf16[128,2,8,128]{3,2,1,0:T(8,128)(2,1)}, u32[]{:S(2)}) %copy-start.2) | copy-done | bytes 524312
  4.0 0.0 copy-start.3
  4.0 0.9 %copy-done.3 = bf16[4,16,2,8,128]{4,3,2,1,0:T(8,128)(2,1)S(1)} copy-done((bf16[4,16,2,8,128]{4,3,2,1,0:T(8,128)(2,1)S(1)}, bf16[4,16,2,8,128]{4,3,2,1,0:T(8,128)(2,1)}, u32[]{:S(2)}) %copy-start.3) | copy-done | bytes 262168
  5.0 0.0 copy-start.4
  5.0 0.9 %copy-done.4 = bf16[512,2,128]{2,1,0:T(2,128)(2,1)S(1)} copy-done((bf16[512,2,128]{2,1,0:T(2,128)(2,1)S(1)}, bf16[512,2,128]{2,1,0:T(2,128)(2,1)}, u32[]{:S(2)}) %copy-start.4) | copy-done | bytes 262168
  5.9 0.0 copy-start.5
  5.9 0.9 %copy-done.5 = bf16[512,2,128]{2,1,0:T(2,128)(2,1)S(1)} copy-done((bf16[512,2,128]{2,1,0:T(2,128)(2,1)S(1)}, bf16[512,2,128]{2,1,0:T(2,128)(2,1)}, u32[]{:S(2)}) %copy-start.5) | copy-done | bytes 262168
  6.9 0.0 copy-start.6
  6.9 0.9 %copy-done.6 = bf16[128,2,2,128]{3,2,1,0:T(2,128)(2,1)S(1)} copy-done((bf16[128,2,2,128]{3,2,1,0:T(2,128)(2,1)S(1)}, bf16[128,2,2,128]{3,2,1,0:T(2,128)(2,1)}, u32[]{:S(2)}) %copy-start.6) | copy-done | bytes 131096
  7.8 0.0 copy-start.7
  7.8 0.8 %copy-done.7 = bf16[4,16,2,2,128]{4,3,2,1,0:T(2,128)(2,1)S(1)} copy-done((bf16[4,16,2,2,128]{4,3,2,1,0:T(2,128)(2,1)S(1)}, bf16[4,16,2,2,128]{4,3,2,1,0:T(2,128)(2,1)}, u32[]{:S(2)}) %copy-start.7) | copy-done | bytes 65560
  8.6 0.0 copy-start.8
  8.6 0.7 %copy-done.8 = s32[1,128]{1,0:T(1,128)S(1)} copy-done((s32[1,128]{1,0:T(1,128)S(1)}, s32[1,128]{1,0:T(1,128)}, u32[]{:S(2)}) %copy-start.8) | copy-done | bytes 536
  9.3 0.0 copy-start.9
  9.3 0.7 %copy-done.9 = s32[4]{0:T(128)S(1)} copy-done((s32[4]{0:T(128)S(1)}, s32[4]{0:T(128)}, u32[]{:S(2)}) %copy-start.9) | copy-done | bytes 40
  10.0 45.1 %shard_map.100 = bf16[2048,128]{1,0:T(8,128)(2,1)S(1)} custom-call(bf16[128,8192]{1,0:T(8,128)(2,1)S(1)} %copy-done, bf16[96,8192]{1,0:T(8,128)(2,1)S(1)} %bitcast.11, bf16[1024,128]{1,0:T(8,128)(2,1)S(1)} %bitcast.13, bf16[256,128]{1,0:T(8,128)(2,1)S(1)} %bitcast.17, bf16[2048,128]{1,0:T(8,128)(2,1)S(1)} %bitcast.12, bf16[512,128]{1,0:T(8,128)(2,1)S(1)} %bitcast.16, ...), custom_call_target="tpu_custom_call" | custom-call | tf_op jit(solution)/shard_map/pallas_call | solution.py:421
  55.1 0.8 %copy.12 = bf16[128,2,8,128]{3,2,1,0:T(8,128)(2,1)} copy(bf16[128,2,8,128]{3,2,1,0:T(8,128)(2,1)S(1)} %bitcast.10) | data formatting | bytes 1048576
Async XLA Ops:
  0.0 1.6 %copy-start = (bf16[128,8192]{1,0:T(8,128)(2,1)S(1)}, bf16[128,8192]{1,0:T(8,128)(2,1)}, u32[]{:S(2)}) copy-start(bf16[128,8192]{1,0:T(8,128)(2,1)} %tok_hbm.1) | copy-start | bytes 6291460
  1.6 1.4 %copy-start.1 = (bf16[2,8192,48]{1,2,0:T(8,128)(2,1)S(1)}, bf16[2,8192,48]{1,2,0:T(8,128)(2,1)}, u32[]{:S(2)}) copy-start(bf16[2,8192,48]{1,2,0:T(8,128)(2,1)} %param.11) | copy-start | bytes 4718596
  3.0 1.0 %copy-start.2 = (bf16[128,2,8,128]{3,2,1,0:T(8,128)(2,1)S(1)}, bf16[128,2,8,128]{3,2,1,0:T(8,128)(2,1)}, u32[]{:S(2)}) copy-start(bf16[128,2,8,128]{3,2,1,0:T(8,128)(2,1)} %param.14) | copy-start | bytes 1572868
  4.0 0.9 %copy-start.3 = (bf16[4,16,2,8,128]{4,3,2,1,0:T(8,128)(2,1)S(1)}, bf16[4,16,2,8,128]{4,3,2,1,0:T(8,128)(2,1)}, u32[]{:S(2)}) copy-start(bf16[4,16,2,8,128]{4,3,2,1,0:T(8,128)(2,1)} %param.12) | copy-start | bytes 786436
  5.0 0.9 %copy-start.4 = (bf16[512,2,128]{2,1,0:T(2,128)(2,1)S(1)}, bf16[512,2,128]{2,1,0:T(2,128)(2,1)}, u32[]{:S(2)}) copy-start(bf16[512,2,128]{2,1,0:T(2,128)(2,1)} %param.16) | copy-start | bytes 786436
  5.9 0.9 %copy-start.5 = (bf16[512,2,128]{2,1,0:T(2,128)(2,1)S(1)}, bf16[512,2,128]{2,1,0:T(2,128)(2,1)}, u32[]{:S(2)}) copy-start(bf16[512,2,128]{2,1,0:T(2,128)(2,1)} %param.17) | copy-start | bytes 786436
  6.9 0.9 %copy-start.6 = (bf16[128,2,2,128]{3,2,1,0:T(2,128)(2,1)S(1)}, bf16[128,2,2,128]{3,2,1,0:T(2,128)(2,1)}, u32[]{:S(2)}) copy-start(bf16[128,2,2,128]{3,2,1,0:T(2,128)(2,1)} %param.15) | copy-start | bytes 393220
  7.8 0.8 %copy-start.7 = (bf16[4,16,2,2,128]{4,3,2,1,0:T(2,128)(2,1)S(1)}, bf16[4,16,2,2,128]{4,3,2,1,0:T(2,128)(2,1)}, u32[]{:S(2)}) copy-start(bf16[4,16,2,2,128]{4,3,2,1,0:T(2,128)(2,1)} %param.13) | copy-start | bytes 196612
  8.6 0.7 %copy-start.8 = (s32[1,128]{1,0:T(1,128)S(1)}, s32[1,128]{1,0:T(1,128)}, u32[]{:S(2)}) copy-start(s32[1,128]{1,0:T(1,128)} %slot_hbm.1) | copy-start | bytes 1540
  9.3 0.7 %copy-start.9 = (s32[4]{0:T(128)S(1)}, s32[4]{0:T(128)}, u32[]{:S(2)}) copy-start(s32[4]{0:T(128)} %len_hbm.1) | copy-start | bytes 52
